TPU v7x, 512 devices: a whole 4x4x16 slice. The times are simulated.
512 devices in a mesh: layer: 4 (over y), row: 8 (over x, core), col: 16 (over z).
Axes of the slice: x: 4, y: 4, z: 16, core: 2. Of those that a mesh axis runs over, the one named last changes fastest.
Arguments:
- stiff_blocks: bfloat16 [4, 8, 16, 2, 16, 4096], P('layer', 'row', 'col'), may hold values from -0.19921875 to 0.19921875
- block_pos: int32 [4, 8, 16, 2, 16], P('layer', 'row', 'col'), may hold values from 0 to 31, as said below
- block_count: int32 [4, 8, 16, 2], P('layer', 'row', 'col'), may hold values from 4 to 16
- modes: bfloat16 [4, 2, 4096, 2048], P('layer', None, 'row', 'col'), may hold values from -6 to 6
- panel_owner: int32 [4, 2, 64], P('layer'), may hold values from 0 to 63, each once within a row
Outputs:
- stiff_modes: bfloat16 [4096, 2048], P(('row', 'layer'), 'col')
Inputs may be any that keep to these rules, and one draw needn't show every extreme that they name: `block_pos`: the positions of one piece are all different.
All inputs are finite; a program needn't handle non-finite values.
Results may differ from a plain program's by a relative error of at most 0.011.
Values may be sent and summed in bfloat16 or wider, within the bound.
No kernel may reach another device: no remote copies, remote signals or barrier semaphores. Data moves between devices by JAX's collectives and lax.ppermute only.
A program may use at most 128 MiB of HBM per device.

v0:
```python
import jax
import jax.numpy as jnp
from jax import lax
from jax.sharding import PartitionSpec as P

BLK = 64
KW = 4
STEPS = 2


def densify_many(vals, pos, cnt, width):
    slots = vals.shape[1]
    live = jnp.arange(slots, dtype=jnp.int32)[None, :] < cnt[:, None]
    masked = jnp.where(live[:, :, None], vals, jnp.zeros_like(vals))
    onehot = (jnp.arange(width, dtype=jnp.int32)[None, :, None] == pos[:, None, :]).astype(
        jnp.bfloat16
    )
    filled = jnp.einsum("pwn,pnx->pwx", onehot, masked, preferred_element_type=jnp.float32)
    return filled.astype(jnp.bfloat16)


def permute_panel(gathered, owner, width):
    blocks = gathered.reshape(-1, BLK, width)
    count = blocks.shape[0]
    select = (owner[:, None] == jnp.arange(count, dtype=jnp.int32)[None, :]).astype(jnp.bfloat16)
    moved = jnp.einsum("gp,pbc->gbc", select, blocks, preferred_element_type=jnp.float32)
    return moved.astype(jnp.bfloat16)


def filled_product(filled, panel, brows):
    pieces = filled.shape[0]
    width = panel.shape[2]
    rows = panel.reshape(pieces, KW, BLK, width)
    shaped = filled.reshape(pieces, brows, KW, BLK, BLK)
    out = jnp.einsum("prkab,pkbc->rac", shaped, rows, preferred_element_type=jnp.float32)
    return out.reshape(brows * BLK, width)


def make_sparse_fold(panel, brows):

    def fold(total, pieces, start):
        vals, pos, cnt = pieces
        filled = densify_many(vals, pos, cnt, brows * KW)
        return total + filled_product(filled, panel, brows)

    return fold


def body(stiff_blocks, block_pos, block_count, modes, panel_owner):
    brows = block_pos.shape[4] * 2 // KW
    width = modes.shape[3]
    total = jnp.zeros((brows * BLK, width), jnp.float32)
    for step in range(STEPS):
        gathered = lax.all_gather(modes[0, step], "row", axis=0, tiled=True)
        panel = permute_panel(gathered, panel_owner[0, step], width)
        vals = stiff_blocks[0, 0, :, step]
        pos = block_pos[0, 0, :, step]
        cnt = block_count[0, 0, :, step]
        folder = make_sparse_fold(panel, brows)
        total = folder(
            total,
            (
                lax.all_gather(vals, "col", axis=0, tiled=True),
                lax.all_gather(pos, "col", axis=0, tiled=True),
                lax.all_gather(cnt, "col", axis=0, tiled=True),
            ),
            jnp.int32(0),
        )
    share = lax.psum_scatter(total, "layer", scatter_dimension=0, tiled=True)
    return share.astype(jnp.bfloat16)


def solution(mesh):
    return jax.shard_map(
        body,
        mesh=mesh,
        in_specs=(
            P("layer", "row", "col", None, None, None),
            P("layer", "row", "col", None, None),
            P("layer", "row", "col", None),
            P("layer", None, "row", "col"),
            P("layer", None, None),
        ),
        out_specs=P(("row", "layer"), "col"),
        check_vma=False,
    )
```

profile of v0, /device:TPU:1, one launch (start us, length us, event | category | flops | bytes accessed | tf_op | source)
XLA Modules:
  0.0 305.8 jit_solution(1472881971238711609)
XLA Ops:
  6.5 1.7 fusion.19
  9.1 1.7 fusion.20
  11.4 1.3 dynamic-slice
  12.7 1.3 fusion.22
  15.3 1.4 bitcast_dynamic-update-slice_fusion.1
  16.6 23.8 %all-reduce.2 = (s32[16]{0:T(128)S(1)}, s32[16]{0:T(128)S(1)}) all-reduce(s32[16]{0:T(128)S(1)} %bitcast_dynamic-update-slice_fusion, s32[16]{0:T(128)S(1)} %bitcast_dynamic-update-slice_fusion.1), channel_id=7, replica_groups=mesh['layer'=4,'row'=8,'col'=16] {'col'}, use_global_device_ids=true, to_apply=%add.1 | all-reduce | flops 32 | bytes 256
  41.2 19.5 %all-gather.4 = s32[16,1,1,1,16]{4,3,2,1,0:T(1,128)S(1)} all-gather(s32[1,1,1,1,16]{4,3,2,1,0:T(1,128)S(1)} %get-tuple-element.14), channel_id=6, replica_groups=mesh['layer'=4,'row'=8,'col'=16] {'col'}, dimensions={0}, use_global_device_ids=true | all-gather | bytes 1088 | tf_op jit(solution)/shard_map/all_gather | solution.py:64
  60.7 19.6 %all-gather = s32[16,1,1,1,16]{4,3,2,1,0:T(1,128)S(1)} all-gather(s32[1,1,1,1,16]{4,3,2,1,0:T(1,128)S(1)} %get-tuple-element.13), channel_id=2, replica_groups=mesh['layer'=4,'row'=8,'col'=16] {'col'}, dimensions={0}, use_global_device_ids=true | all-gather | bytes 1088 | tf_op jit(solution)/shard_map/all_gather | solution.py:64
  81.2 2.2 convolution_convert_fusion.2
  83.3 2.2 convolution_convert_fusion.3
  85.5 59.6 %all-gather.17.cloned.1.call-done = bf16[16,1,1,1,16,4096]{5,4,3,2,1,0:T(8,128)(2,1)} async-done(((bf16[1,1,1,1,16,4096]{5,4,3,2,1,0:T(8,128)(2,1)}), bf16[16,1,1,1,16,4096]{5,4,3,2,1,0:T(8,128)(2,1)}) %all-gather.17.cloned.1.call-update) | async-done | bytes 2097168 | tf_op jit(solution)/shard_map/all_gather | solution.py:63
  145.1 4.9 %convolution_convert_fusion = bf16[16,32,4096]{2,1,0:T(8,128)(2,1)} fusion(bf16[16,1,1,1,16,4096]{5,4,3,2,1,0:T(8,128)(2,1)} %all-gather.17.cloned.1.call-done, pred[16,16]{1,0:T(8,128)(4,1)S(1)} %iota_compare_fusion.6, s32[16,16]{1,0:T(8,128)S(1)} %bitcast.56), kind=kOutput, calls=%fused_computation | convolution fusion | flops 70262784 | bytes 6292736 | tf_op jit(solution)/shard_map/pwn,pnx->pwx/dot_general | solution.py:18
  150.0 12.6 %reshape.71 = bf16[16,8,4,64,64]{4,3,2,1,0:T(8,128)(2,1)} reshape(bf16[16,32,4096]{2,1,0:T(8,128)(2,1)} %convolution_convert_fusion) | data formatting | bytes 8388608 | tf_op jit(solution)/shard_map/reshape | solution.py:34
  162.7 12.1 %copy.21 = bf16[8,64,64,4,16]{1,0,2,4,3:T(8,128)(2,1)} copy(bf16[8,64,64,4,16]{2,1,3,0,4:T(8,128)(2,1)} %bitcast.49) | data formatting | bytes 8388608 | tf_op jit(solution)/shard_map/prkab,pkbc->rac/dot_general | solution.py:35
  174.8 11.8 %dot_general.33 = bf16[512,64,4,16]{0,1,3,2:T(8,128)(2,1)} reshape(bf16[8,64,64,4,16]{1,0,2,4,3:T(8,128)(2,1)} %copy.21) | data formatting | bytes 8388608 | tf_op jit(solution)/shard_map/prkab,pkbc->rac/dot_general | solution.py:35
  186.5 30.6 %all-gather.13.cloned.1.call-done = bf16[16,1,1,1,16,4096]{5,4,3,2,1,0:T(8,128)(2,1)} async-done(((bf16[1,1,1,1,16,4096]{5,4,3,2,1,0:T(8,128)(2,1)}), bf16[16,1,1,1,16,4096]{5,4,3,2,1,0:T(8,128)(2,1)}) %all-gather.13.cloned.1.call-update) | async-done | bytes 2097168 | tf_op jit(solution)/shard_map/all_gather | solution.py:63
  217.2 4.9 %convolution_convert_fusion.1 = bf16[16,32,4096]{2,1,0:T(8,128)(2,1)} fusion(bf16[16,1,1,1,16,4096]{5,4,3,2,1,0:T(8,128)(2,1)} %all-gather.13.cloned.1.call-done, pred[16,16]{1,0:T(8,128)(4,1)S(1)} %iota_compare_fusion.7, s32[16,16]{1,0:T(8,128)S(1)} %bitcast.55), kind=kOutput, calls=%fused_computation.1 | convolution fusion | flops 70262784 | bytes 6292736 | tf_op jit(solution)/shard_map/pwn,pnx->pwx/dot_general | solution.py:18
  222.1 12.6 %reshape.68 = bf16[16,8,4,64,64]{4,3,2,1,0:T(8,128)(2,1)} reshape(bf16[16,32,4096]{2,1,0:T(8,128)(2,1)} %convolution_convert_fusion.1) | data formatting | bytes 8388608 | tf_op jit(solution)/shard_map/reshape | solution.py:34
  234.7 12.1 %copy.18 = bf16[8,64,64,4,16]{1,0,2,4,3:T(8,128)(2,1)} copy(bf16[8,64,64,4,16]{2,1,3,0,4:T(8,128)(2,1)} %bitcast.50) | data formatting | bytes 8388608 | tf_op jit(solution)/shard_map/prkab,pkbc->rac/dot_general | solution.py:35
  246.8 11.8 %dot_general.28 = bf16[512,64,4,16]{0,1,3,2:T(8,128)(2,1)} reshape(bf16[8,64,64,4,16]{1,0,2,4,3:T(8,128)(2,1)} %copy.18) | data formatting | bytes 8388608 | tf_op jit(solution)/shard_map/prkab,pkbc->rac/dot_general | solution.py:35
  258.6 4.2 %convolution_bitcast_fusion = f32[512,128]{1,0:T(8,128)S(1)} fusion(bf16[512,64,4,16]{0,1,3,2:T(8,128)(2,1)} %dot_general.33, bf16[16,4,64,128]{3,1,0,2:T(4,128)(2,1)S(1)} %bitcast.53), kind=kOutput, calls=%fused_computation.8 | convolution fusion | flops 536870912 | bytes 5505024 | tf_op jit(solution)/shard_map/prkab,pkbc->rac/dot_general | solution.py:35
  262.8 2.8 fusion.2
  265.6 32.2 %reduce-scatter.2.cloned.1.call-done = f32[128,128]{1,0:T(8,128)} async-done(((f32[512,128]{1,0:T(8,128)}), f32[128,128]{1,0:T(8,128)}) %reduce-scatter.2.cloned.1.call-update) | async-done | bytes 65552 | tf_op jit(solution)/shard_map/reduce_scatter | solution.py:69
  297.9 1.5 convert_element_type.23
  (21 shorter events, 4.3 us)
Async XLA Ops:
  6.5 74.6 %all-gather.19.cloned.1.call-start = ((), (), s32[]{:S(2)}) async-start(), calls=%async_computation.5 | async-start | bytes 1179648 | tf_op jit(solution)/shard_map/all_gather | solution.py:54
  8.3 75.1 %all-gather.15.cloned.1.call-start = ((), (), s32[]{:S(2)}) async-start(), calls=%async_computation.3 | async-start | bytes 1179648 | tf_op jit(solution)/shard_map/all_gather | solution.py:54
  9.0 136.1 %all-gather.17.cloned.1.call-start = ((), (), s32[]{:S(2)}) async-start(), calls=%async_computation.4 | async-start | bytes 2228224 | tf_op jit(solution)/shard_map/all_gather | solution.py:63
  10.8 206.4 %all-gather.13.cloned.1.call-start = ((), (), s32[]{:S(2)}) async-start(), calls=%async_computation.2 | async-start | bytes 2228224 | tf_op jit(solution)/shard_map/all_gather | solution.py:63
  11.4 286.5 %reduce-scatter.2.cloned.1.call-start = ((), (), s32[]{:S(2)}) async-start(), calls=%async_computation.1 | async-start | bytes 327680 | tf_op jit(solution)/shard_map/reduce_scatter | solution.py:69
  258.5 4.2 %copy-start = (bf16[512,64,4,16]{0,1,3,2:T(8,128)(2,1)S(1)}, bf16[512,64,4,16]{0,1,3,2:T(8,128)(2,1)}, u32[]{:S(2)}) copy-start(bf16[512,64,4,16]{0,1,3,2:T(8,128)(2,1)} %dot_general.28) | copy-start | bytes 12582916
Sparse Core Ops, SparseCore 0:
  9.5 36.7 all-gather.18
  48.4 31.1 all-gather.14
  81.7 63.3 all-gather.16
  147.1 70.0 all-gather.12
  265.7 32.0 reduce-scatter.1
where the time goes:
time: 309 us; the launch traced here: 306 us
  waiting for transfers between devices  124 us (40%)
  local copies, waits for them, and re-layouts  83.1 us (27%)
  blocking collectives  62.8 us (20%)
  matrix products  21.2 us (7%)
  between operations  13.2 us (4%)
    all_gather x2, waiting for transfers between devices, body(): lax.all_gather(vals, 'col', axis=0, tiled=True)  90.2 us
    dot_general x4, local copies, waits for them, and re-layouts, filled_product(): jnp.einsum('prkab,pkbc->rac', shaped, rows, preferred_element_type=jnp.fl...  47.8 us
    all_gather x2, blocking collectives, body(): lax.all_gather(pos, 'col', axis=0, tiled=True)  39 us
    reduce_scatter x1, waiting for transfers between devices, body(): share = lax.psum_scatter(total, 'layer', scatter_dimension=0, tiled=True)  32.2 us
    reshape x2, local copies, waits for them, and re-layouts, filled_product(): shaped = filled.reshape(pieces, brows, KW, BLK, BLK)  25.2 us
    unnamed x1, blocking collectives  23.8 us
    dot_general x2, matrix products, densify_many(): jnp.einsum('pwn,pnx->pwx', onehot, masked, preferred_element_type=jnp.flo...  9.85 us
    dot_general x2, matrix products, filled_product(): jnp.einsum('prkab,pkbc->rac', shaped, rows, preferred_element_type=jnp.fl...  7.04 us
  transfers between devices with their start and end apart: 5, of which 3 were waited for; matrix products, arithmetic and copies ran while one was open for 18% of the time, Pallas kernels for 0%

commit v1 on v0

v1 whole, which is shorter than its diff:
```python
import jax
import jax.numpy as jnp
from jax import lax
from jax.experimental import pallas as pl
from jax.experimental.pallas import tpu as pltpu
from jax.sharding import PartitionSpec as P

BLK = 64
KW = 4
STEPS = 2
LANES = 128
NCH = 4


def fill_rhs(rhs_ref, b_ref, own_ref, s, g0, row0, blks):
    for bc in range(KW):
        p = own_ref[s, g0 + bc]
        blk = b_ref[((p // blks) * STEPS + s) * blks + p % blks]
        for h in range(2):
            r = row0 + bc * LANES + h * BLK
            rhs_ref[r : r + BLK, h * LANES : (h + 1) * LANES] = blk


def fill_lhs(lhs_ref, raw, spot, col0, brows):
    slots = raw.shape[0]
    tiles = raw.shape[1] // LANES
    ids = lax.broadcasted_iota(jnp.int32, (KW * brows, slots), 0)
    onehot = jnp.where(ids == spot, 1.0, 0.0).astype(jnp.bfloat16)
    dense = jnp.dot(onehot, raw, preferred_element_type=jnp.float32)
    for bc in range(KW):
        cols = jnp.concatenate(
            [
                dense[bc * brows : (bc + 1) * brows, k * LANES : (k + 1) * LANES]
                for k in range(tiles)
            ],
            axis=0,
        )
        lhs_ref[:, col0 + bc * LANES : col0 + (bc + 1) * LANES] = cols.astype(jnp.bfloat16)


def product_kernel(own_ref, a_ref, spot_ref, b_ref, out_ref, lhs_ref, rhs_ref, acc_ref, *, brows, blks):
    step = pl.program_id(0)
    per = a_ref.shape[0]
    width = KW * LANES

    @pl.when(step == 0)
    def _():
        rhs_ref[...] = jnp.zeros_like(rhs_ref)
        acc_ref[...] = jnp.zeros_like(acc_ref)

    def one(i, carry):
        c = step * per + i
        for s in range(STEPS):
            fill_lhs(lhs_ref, a_ref[i, s], spot_ref[i, s : s + 1, :], s * width, brows)
            fill_rhs(rhs_ref, b_ref, own_ref, s, c * KW, s * width, blks)
        more = jnp.dot(lhs_ref[...], rhs_ref[...], preferred_element_type=jnp.float32)
        for h in range(2):
            acc_ref[h] += more[:, h * LANES : (h + 1) * LANES]
        return carry

    lax.fori_loop(0, per, one, 0)

    @pl.when(step == pl.num_programs(0) - 1)
    def _():
        layers = out_ref.shape[0]
        per_layer = brows // layers
        tiles = acc_ref.shape[1] // brows
        for l in range(layers):
            for j in range(per_layer):
                for h in range(2):
                    out_ref[l, j * tiles : (j + 1) * tiles, h * LANES : (h + 1) * LANES] = acc_ref[
                        h, pl.ds(l * per_layer + j, tiles, stride=brows), :
                    ]


def finish_kernel(parts_ref, out_ref, rows_ref):
    total = jnp.sum(parts_ref[...], axis=0)
    tiles = BLK // 2
    for j in range(total.shape[0] // tiles):
        for h in range(2):
            rows_ref[pl.ds(j * BLK + h, tiles, stride=2), :] = total[
                j * tiles : (j + 1) * tiles, h * LANES : (h + 1) * LANES
            ]
    out_ref[...] = rows_ref[...].astype(jnp.bfloat16)


def body(stiff_blocks, block_pos, block_count, modes, panel_owner):
    layers = lax.axis_size("layer")
    rows_n = lax.axis_size("row")
    cols_n = lax.axis_size("col")
    slots = stiff_blocks.shape[4]
    brows = slots * 2 // KW
    width = modes.shape[3]
    depth = modes.shape[2]
    blks = depth // BLK

    slot_ids = jnp.arange(slots, dtype=jnp.int32)
    live = slot_ids[None, :] < block_count[0, 0, 0][:, None]
    pos = block_pos[0, 0, 0]
    spot = jnp.where(live, (pos % KW) * brows + pos // KW, KW * brows)

    a = lax.all_gather(stiff_blocks[0, 0], "col", axis=0, tiled=True)
    spot = lax.all_gather(spot, "col", axis=0, tiled=False)

    flat = modes.reshape(STEPS * depth, width)
    cut = STEPS * depth // NCH
    parts = [
        lax.all_gather(flat[i * cut : (i + 1) * cut], "row", axis=0, tiled=False) for i in range(NCH)
    ]
    b = jnp.concatenate(parts, axis=1).reshape(rows_n * STEPS * blks, BLK, width)

    per = 4
    tiles = BLK * BLK // LANES
    parts = pl.pallas_call(
        lambda *refs: product_kernel(*refs, brows=brows, blks=blks),
        grid_spec=pltpu.PrefetchScalarGridSpec(
            num_scalar_prefetch=1,
            grid=(cols_n // per,),
            in_specs=[
                pl.BlockSpec((per, STEPS, slots, BLK * BLK), lambda i, o: (i, 0, 0, 0)),
                pl.BlockSpec((per, STEPS, slots), lambda i, o: (i, 0, 0)),
                pl.BlockSpec((rows_n * STEPS * blks, BLK, width), lambda i, o: (0, 0, 0)),
            ],
            out_specs=pl.BlockSpec((layers, brows * tiles // layers, 2 * LANES), lambda i, o: (0, 0, 0)),
            scratch_shapes=[
                pltpu.VMEM((brows * tiles, STEPS * KW * LANES), jnp.bfloat16),
                pltpu.VMEM((STEPS * KW * LANES, 2 * LANES), jnp.bfloat16),
                pltpu.VMEM((2, brows * tiles, LANES), jnp.float32),
            ],
        ),
        out_shape=jax.ShapeDtypeStruct((layers, brows * tiles // layers, 2 * LANES), jnp.float32),
        compiler_params=pltpu.CompilerParams(vmem_limit_bytes=40 * 1024 * 1024),
        name="product",
    )(panel_owner[0], a, spot, b)
    parts = lax.all_to_all(parts, "layer", 0, 0, tiled=True)
    return pl.pallas_call(
        finish_kernel,
        out_shape=jax.ShapeDtypeStruct((brows * BLK // layers, width), jnp.bfloat16),
        scratch_shapes=[pltpu.VMEM((brows * BLK // layers, width), jnp.float32)],
        name="finish",
    )(parts)


def solution(mesh):
    return jax.shard_map(
        body,
        mesh=mesh,
        in_specs=(
            P("layer", "row", "col", None, None, None),
            P("layer", "row", "col", None, None),
            P("layer", "row", "col", None),
            P("layer", None, "row", "col"),
            P("layer", None, None),
        ),
        out_specs=P(("row", "layer"), "col"),
        check_vma=False,
    )
```

time: 309 us -> 129 us (0.42)
  waiting for transfers between devices: 124 us -> 0.73 us
  local copies, waits for them, and re-layouts: 83.1 us -> 3.15 us
  blocking collectives: 62.8 us -> 99.9 us
  matrix products: 21.2 us -> 0 us
  Pallas kernels: 0 us -> 10.1 us
    all_gather x4 -> x1, waiting for transfers between devices: 90.3 us -> 0.02 us  [body(): a = lax.all_gather(stiff_blocks[0, 0], 'col', axis=0, tiled=True)]
    all_gather x2 -> x5, blocking collectives: 39 us -> 89.5 us  [the longest x4 59.4 us: body(): lax.all_gather(flat[i * cut:(i + 1) * cut], 'row', axis=0, tiled=False)]
    dot_general x4 -> x0, local copies, waits for them, and re-layouts: 47.8 us -> none  [filled_product(): jnp.einsum('prkab,pkbc->rac', shaped, rows, preferred_element_type=jnp.fl...]
    reduce_scatter x1 -> x0, waiting for transfers between devices: 32.2 us -> none  [body(): share = lax.psum_scatter(total, 'layer', scatter_dimension=0, tiled=True)]
    reshape x2 -> x0, local copies, waits for them, and re-layouts: 25.2 us -> none  [filled_product(): shaped = filled.reshape(pieces, brows, KW, BLK, BLK)]
    unnamed x1 -> x0, blocking collectives: 23.8 us -> none
    dot_general x6 -> x0, matrix products: 21.2 us -> none  [the longest x2 9.85 us: densify_many(): jnp.einsum('pwn,pnx->pwx', onehot, masked, preferred_element_type=jnp.flo...]
    all_to_all x0 -> x1, blocking collectives: none -> 10.4 us  [body(): parts = lax.all_to_all(parts, 'layer', 0, 0, tiled=True)]
  transfers between devices with their start and end apart: 5 -> 1, of which waited for: 3 -> 0; matrix products, arithmetic and copies ran while one was open for 18% -> 1% of each run, Pallas kernels for 0% -> 0%
where the time goes in v1:
time: 129 us; the launch traced here: 128 us
  blocking collectives  99.9 us (77%)
  between operations  13.4 us (10%)
  Pallas kernels  10.1 us (8%)
  local copies, waits for them, and re-layouts  3.15 us (2%)
    all_gather x4, blocking collectives, body(): lax.all_gather(flat[i * cut:(i + 1) * cut], 'row', axis=0, tiled=False)  59.4 us
    all_gather x1, blocking collectives, body(): spot = lax.all_gather(spot, 'col', axis=0, tiled=False)  30.1 us
    all_to_all x1, blocking collectives, body(): parts = lax.all_to_all(parts, 'layer', 0, 0, tiled=True)  10.4 us
    pallas_call x1, Pallas kernels, body(): pl.pallas_call(lambda *refs: product_kernel(*refs, brows=brows, blks=blks...  8.48 us
  transfers between devices with their start and end apart: 1, of which 0 were waited for; matrix products, arithmetic and copies ran while one was open for 1% of the time, Pallas kernels for 0%

profile of v1, /device:TPU:1, one launch (start us, length us, event | category | flops | bytes accessed | tf_op | source)
XLA Modules:
  0.0 128.2 jit_solution(6761160572943376740)
XLA Ops:
  6.5 0.0 copy-start.1
  6.5 0.0 all-gather.7.cloned.1.call-start
  6.5 0.7 all-gather.7.cloned.1.call-update
  7.3 0.8 compare_select_fusion
  8.0 30.1 %all_gather.32.refs_2_ = s32[16,2,16]{2,1,0:T(2,128)S(1)} all-gather(s32[1,2,16]{2,1,0:T(2,128)S(1)} %compare_select_fusion), channel_id=1, replica_groups=mesh['layer'=4,'row'=8,'col'=16] {'col'}, dimensions={0}, use_global_device_ids=true | all-gather | bytes 2176 | tf_op jit(solution)/shard_map/all_gather | solution.py:103
  38.1 1.0 fusion.2
  39.1 20.1 %all-gather.1 = bf16[2048,128]{1,0:T(8,128)(2,1)S(1)} all-gather(bf16[256,128]{1,0:T(8,128)(2,1)S(1)} %get-tuple-element.5), channel_id=3, replica_groups=mesh['layer'=4,'row'=8,'col'=16] {'row'}, dimensions={0}, use_global_device_ids=true | all-gather | bytes 589824 | tf_op jit(solution)/shard_map/all_gather | solution.py:108
  59.2 13.1 %all-gather.2 = bf16[2048,128]{1,0:T(8,128)(2,1)S(1)} all-gather(bf16[256,128]{1,0:T(8,128)(2,1)S(1)} %get-tuple-element.8), channel_id=4, replica_groups=mesh['layer'=4,'row'=8,'col'=16] {'row'}, dimensions={0}, use_global_device_ids=true | all-gather | bytes 589824 | tf_op jit(solution)/shard_map/all_gather | solution.py:108
  72.3 13.1 %all-gather.3 = bf16[2048,128]{1,0:T(8,128)(2,1)S(1)} all-gather(bf16[256,128]{1,0:T(8,128)(2,1)S(1)} %get-tuple-element.7), channel_id=5, replica_groups=mesh['layer'=4,'row'=8,'col'=16] {'row'}, dimensions={0}, use_global_device_ids=true | all-gather | bytes 589824 | tf_op jit(solution)/shard_map/all_gather | solution.py:108
  85.4 13.1 %all-gather.4 = bf16[2048,128]{1,0:T(8,128)(2,1)S(1)} all-gather(bf16[256,128]{1,0:T(8,128)(2,1)S(1)} %get-tuple-element.6), channel_id=6, replica_groups=mesh['layer'=4,'row'=8,'col'=16] {'row'}, dimensions={0}, use_global_device_ids=true | all-gather | bytes 589824 | tf_op jit(solution)/shard_map/all_gather | solution.py:108
  98.5 0.1 pad_maximum_fusion
  98.6 0.0 all-gather.7.cloned.1.call-done
  98.7 0.0 copy-done.1
  98.7 0.0 copy-start
  98.7 2.2 %copy-done = bf16[16,1,1,2,16,4096]{5,4,3,2,1,0:T(8,128)(2,1)S(1)} copy-done((bf16[16,1,1,2,16,4096]{5,4,3,2,1,0:T(8,128)(2,1)S(1)}, bf16[16,1,1,2,16,4096]{5,4,3,2,1,0:T(8,128)(2,1)}, u32[]{:S(2)}) %copy-start) | copy-done | bytes 4194328
  100.9 8.5 %product.1 = f32[4,64,256]{2,1,0:T(8,128)S(1)} custom-call(s32[2,64]{1,0:T(2,128)S(1)} %bitcast.19, bf16[16,2,16,4096]{3,2,1,0:T(8,128)(2,1)S(1)} %bitcast.18, s32[16,2,16]{2,1,0:T(2,128)S(1)} %all_gather.32.refs_2_, bf16[128,64,128]{2,1,0:T(8,128)(2,1)S(1)} %bitcast.17), custom_call_target="tpu_custom_call" | custom-call | tf_op jit(solution)/shard_map/product/pallas_call | solution.py:114
  109.3 10.4 %all_to_all.5.parts_ref = f32[4,64,256]{2,1,0:T(8,128)} all-to-all(f32[4,64,256]{2,1,0:T(8,128)S(1)} %product.1), channel_id=1, replica_groups=mesh['layer'=4,'row'=8,'col'=16] {'layer'}, dimensions={0} | all-to-all | bytes 524288 | tf_op jit(solution)/shard_map/all_to_all | solution.py:135
  119.8 1.6 %finish.1 = bf16[128,128]{1,0:T(8,128)(2,1)} custom-call(f32[4,64,256]{2,1,0:T(8,128)} %all_to_all.5.parts_ref), custom_call_target="tpu_custom_call" | custom-call | tf_op jit(solution)/shard_map/finish/pallas_call | solution.py:136
Async XLA Ops:
  6.5 92.1 %copy-start.1 = (s32[1,2,64]{2,1,0:T(2,128)S(1)}, s32[1,2,64]{2,1,0:T(2,128)}, u32[]{:S(2)}) copy-start(s32[1,2,64]{2,1,0:T(2,128)} %param.9) | copy-start | bytes 1540
  6.5 92.1 %all-gather.7.cloned.1.call-start = ((), (), s32[]{:S(2)}) async-start(), calls=%async_computation.1 | async-start | bytes 4456448 | tf_op jit(solution)/shard_map/all_gather | solution.py:102
  98.7 2.2 %copy-start = (bf16[16,1,1,2,16,4096]{5,4,3,2,1,0:T(8,128)(2,1)S(1)}, bf16[16,1,1,2,16,4096]{5,4,3,2,1,0:T(8,128)(2,1)}, u32[]{:S(2)}) copy-start(bf16[16,1,1,2,16,4096]{5,4,3,2,1,0:T(8,128)(2,1)} %all-gather.7.cloned.1.call-done) | copy-start | bytes 12582916
Sparse Core Ops, SparseCore 0:
  9.4 75.5 all-gather.6

commit v2 on v0

v2 whole, which is shorter than its diff:
```python
import functools

import jax
import jax.numpy as jnp
from jax import lax
from jax.experimental import pallas as pl
from jax.experimental.pallas import tpu as pltpu
from jax.sharding import Mesh, PartitionSpec as P

BLK = 64
KW = 4
STEPS = 2
LANES = 128
TILES = BLK * BLK // LANES
FLAT = BLK * BLK
GROUP = 2


def product_kernel(*refs, parts, brows, slots, blks, group, first, last):
    own_ref, num_ref = refs[0], refs[1]
    count = max(ref for part in parts for ref, _ in part) + 1
    piece_refs = refs[2 : 2 + count]
    rest = refs[2 + count :]
    b_refs, rest = rest[:2], rest[2:]
    if not first:
        acc_in, rest = rest[0], rest[1:]
    out_ref, stage_ref, hot_ref, lhs_ref, rhs_ref, b_ref, sem = rest[:7]
    acc_ref = rest[7] if last else out_ref
    n = len(parts)
    width = KW * LANES
    chunk = group * LANES
    per_b = b_ref.shape[0] // 2

    copies = [
        pltpu.make_async_copy(b_refs[e], b_ref.at[pl.ds(e * per_b, per_b)], sem.at[e]) for e in range(2)
    ]
    for copy in copies:
        copy.start()
    for i, part in enumerate(parts):
        for s in range(STEPS):
            ref, off = part[s]
            stage_ref[i, s] = piece_refs[ref][:, off : off + FLAT]
            ref, off = part[STEPS]
            spot = piece_refs[ref][:, off : off + LANES].astype(jnp.float32)[s : s + 1, :slots]
            ids = lax.broadcasted_iota(jnp.int32, (KW * brows, slots), 0).astype(jnp.float32)
            hot_ref[i, s] = jnp.where(ids == spot, 1.0, 0.0).astype(jnp.bfloat16)
    rhs_ref[...] = jnp.zeros_like(rhs_ref)
    if first:
        acc_ref[...] = jnp.zeros_like(acc_ref)
    else:
        acc_ref[...] = acc_in[...]
    x, core = num_ref[n], num_ref[n + 1]
    for copy in copies:
        copy.wait()

    def one(i, carry):
        g0 = num_ref[i] * KW
        for s in range(STEPS):
            dense = jnp.dot(hot_ref[i, s], stage_ref[i, s], preferred_element_type=jnp.float32)
            for bc in range(KW):
                cols = jnp.concatenate(
                    [
                        dense[bc * brows : (bc + 1) * brows, k * LANES : (k + 1) * LANES]
                        for k in range(TILES)
                    ],
                    axis=0,
                )
                lhs_ref[:, s * width + bc * LANES : s * width + (bc + 1) * LANES] = cols.astype(jnp.bfloat16)
                p = own_ref[s, g0 + bc]
                row = p // blks
                side = (row % 2 + core) % 2
                ahead = (row // 2 + 4 - x) % 4
                for j in range(group):
                    at = (((side * 4 + ahead) * group + j) * STEPS + s) * blks + p % blks
                    blk = b_ref[at]
                    for h in range(2):
                        r = s * width + bc * LANES + h * BLK
                        c = h * chunk + j * LANES
                        rhs_ref[r : r + BLK, c : c + LANES] = blk
        more = jnp.dot(lhs_ref[...], rhs_ref[...], preferred_element_type=jnp.float32)
        for q in range(2 * group):
            acc_ref[q] += more[:, q * LANES : (q + 1) * LANES]
        return carry

    lax.fori_loop(0, n, one, 0)

    if last:
        zc = num_ref[n + 2]
        per_layer = out_ref.shape[1] // TILES
        layers = brows // per_layer
        for l in range(layers):
            for j in range(group):
                to = l * group + (zc + j) % group
                for m in range(per_layer):
                    for h in range(2):
                        out_ref[to, m * TILES : (m + 1) * TILES, h * LANES : (h + 1) * LANES] = acc_ref[
                            h * group + j, pl.ds(l * per_layer + m, TILES, stride=brows), :
                        ]


def product(own, nums, pieces, parts, b, acc, *, brows, slots, blks, layers, last):
    group = GROUP
    n = len(parts)
    first = acc is None
    rows = brows * TILES
    sums = jax.ShapeDtypeStruct((2 * group, rows, LANES), jnp.float32)
    outs = jax.ShapeDtypeStruct((layers * group, rows // layers, 2 * LANES), jnp.float32)
    vmem = pl.BlockSpec(memory_space=pltpu.VMEM)
    smem = pl.BlockSpec(memory_space=pltpu.SMEM)
    scratch = [
        pltpu.VMEM((n, STEPS, slots, FLAT), jnp.bfloat16),
        pltpu.VMEM((n, STEPS, KW * brows, slots), jnp.bfloat16),
        pltpu.VMEM((rows, STEPS * KW * LANES), jnp.bfloat16),
        pltpu.VMEM((STEPS * KW * LANES, 2 * group * LANES), jnp.bfloat16),
        pltpu.VMEM((2 * b[0].shape[0], BLK, LANES), jnp.bfloat16),
        pltpu.SemaphoreType.DMA((2,)),
    ]
    if last:
        scratch.append(pltpu.VMEM(sums.shape, jnp.float32))
    macs = n * STEPS * KW * LANES * rows * 2 * group * LANES
    return pl.pallas_call(
        functools.partial(
            product_kernel, parts=parts, brows=brows, slots=slots, blks=blks, group=group, first=first, last=last
        ),
        in_specs=[smem, smem] + [vmem] * len(pieces) + [pl.BlockSpec(memory_space=pl.ANY)] * 2 + [vmem] * (not first),
        out_specs=vmem,
        scratch_shapes=scratch,
        out_shape=outs if last else sums,
        compiler_params=pltpu.CompilerParams(vmem_limit_bytes=48 * 1024 * 1024),
        cost_estimate=pl.CostEstimate(flops=2 * macs, bytes_accessed=8 << 20, transcendentals=0),
        name="product_last" if last else "product",
    )(own, nums, *pieces, *b, *([] if first else [acc]))


def pack_kernel(stiff_ref, pos_ref, count_ref, out_ref, row_ref, *, brows):
    steps, slots, flat = stiff_ref.shape
    for s in range(steps):
        out_ref[:, s * flat : (s + 1) * flat] = stiff_ref[s]
    row_ref[...] = jnp.zeros_like(row_ref)
    for s in range(steps):
        pos = pos_ref[s : s + 1, :]
        ids = lax.broadcasted_iota(jnp.int32, pos.shape, 1)
        spot = jnp.where(ids < count_ref[s], (pos % KW) * brows + pos // KW, KW * brows)
        row_ref[s : s + 1, 0:slots] = spot.astype(jnp.float32)
    out_ref[:, steps * flat :] = row_ref[...].astype(jnp.bfloat16)


def finish_kernel(parts_ref, out_ref, rows_ref):
    total = jnp.sum(parts_ref[...], axis=0)
    for j in range(total.shape[0] // TILES):
        for h in range(2):
            rows_ref[pl.ds(j * BLK + h, TILES, stride=2), :] = total[
                j * TILES : (j + 1) * TILES, h * LANES : (h + 1) * LANES
            ]
    out_ref[...] = rows_ref[...].astype(jnp.bfloat16)


def body(stiff_blocks, block_pos, block_count, modes, panel_owner):
    layers, nx, nz = lax.axis_size("layer"), lax.axis_size("x"), lax.axis_size("zb")
    x, core, zb, zc = (lax.axis_index(a) for a in ("x", "core", "zb", "zc"))
    slots = stiff_blocks.shape[4]
    brows = slots * 2 // KW
    width = modes.shape[3]
    depth = modes.shape[2]
    blks = depth // BLK

    def turn(v, k):
        pairs = [(c * nz + i, c * nz + (i + (k if c == 0 else -k)) % nz) for c in range(2) for i in range(nz)]
        return lax.ppermute(v, ("core", "zb"), pairs)

    own_piece = pl.pallas_call(
        functools.partial(pack_kernel, brows=brows),
        out_shape=jax.ShapeDtypeStruct((slots, STEPS * FLAT + LANES), jnp.bfloat16),
        scratch_shapes=[pltpu.VMEM((slots, LANES), jnp.float32)],
        in_specs=[pl.BlockSpec(memory_space=pltpu.VMEM)] * 2 + [pl.BlockSpec(memory_space=pltpu.SMEM)],
        name="pack",
    )(stiff_blocks[0, 0, 0], block_pos[0, 0, 0], block_count[0, 0, 0])

    half = nz // 2
    fwd, back = [own_piece], [own_piece]

    def after(value, *others):
        return lax.optimization_barrier((value, *others))

    mine = modes.reshape(STEPS * depth, width)
    far = lax.ppermute(mine, "zc", [(0, 1), (1, 0)])
    fwd.append(turn(fwd[0], 1))
    back[0], far = after(back[0], far)
    mine = jnp.concatenate([mine, far], axis=0)
    moved = [lax.ppermute(mine, "x", [(i, (i - k) % nx) for i in range(nx)]) for k in range(1, nx)]
    back.append(turn(back[0], -1))
    fwd.append(turn(fwd[1], 1))
    back[1], fwd[1] = after(back[1], fwd[1])
    back.append(turn(back[1], -1))
    fwd[2], back[1], *moved = after(fwd[2], back[1], *moved)
    fwd.append(turn(fwd[2], 1))
    back[2], fwd[2] = after(back[2], fwd[2])
    back.append(turn(back[2], -1))
    mine = jnp.concatenate([mine] + moved, axis=0)
    other = lax.ppermute(mine, "core", [(0, 1), (1, 0)])
    fwd[3], back[2], other = after(fwd[3], back[2], other)
    b = [v.reshape(-1, BLK, width) for v in (mine, other)]
    far_end = turn(fwd[3], 1)

    def number(away):
        sign = 1 - 2 * core
        return ((zb - sign * away) % nz) * GROUP + zc

    whole = lambda i: ((i, 0), (i, FLAT), (i, 2 * FLAT))
    own = panel_owner[0]
    call = functools.partial(product, brows=brows, slots=slots, blks=blks, layers=layers)

    def nums(aways):
        return jnp.stack([number(a) for a in aways] + [x, core, zc]).astype(jnp.int32)

    pieces, aways = [own_piece], [0]
    for i in range(1, half - 1):
        pieces += [fwd[i], back[i]]
        aways += [i, -i]
    acc = call(own, nums(aways), pieces, [whole(i) for i in range(len(pieces))], b, None, last=False)
    i = half - 1
    out = call(own, nums([i, -i, half]), [fwd[i], back[i], far_end], [whole(k) for k in range(3)], b, acc, last=True)
    out = lax.all_to_all(out, ("layer", "zc"), 0, 0, tiled=True)
    return pl.pallas_call(
        finish_kernel,
        out_shape=jax.ShapeDtypeStruct((brows * BLK // layers, width), jnp.bfloat16),
        scratch_shapes=[pltpu.VMEM((brows * BLK // layers, width), jnp.float32)],
        name="finish",
    )(out)


def solution(mesh):
    layers, rows, cols = (mesh.shape[a] for a in ("layer", "row", "col"))
    fine = Mesh(
        mesh.devices.reshape(layers, rows // 2, 2, cols // GROUP, GROUP), ("layer", "x", "core", "zb", "zc")
    )
    row, col = ("x", "core"), ("zb", "zc")
    return jax.shard_map(
        body,
        mesh=fine,
        in_specs=(
            P("layer", row, col, None, None, None),
            P("layer", row, col, None, None),
            P("layer", row, col, None),
            P("layer", None, row, col),
            P("layer", None, None),
        ),
        out_specs=P(row + ("layer",), col),
        check_vma=False,
    )
```

time: 309 us -> 106 us (0.34)
  the two profiles are of different devices: /device:TPU:1 before, /device:TPU:2 now
where the time goes in v2:
time: 106 us
  starting transfers between devices  52.5 us (50%)
  waiting for transfers between devices  21 us (20%)
  blocking collectives  15.1 us (14%)
  Pallas kernels  11.3 us (11%)
  local copies, waits for them, and re-layouts  4.31 us (4%)
    ppermute x7, starting transfers between devices, turn(): return lax.ppermute(v, ('core', 'zb'), pairs)  33 us
    ppermute x7, waiting for transfers between devices, turn(): return lax.ppermute(v, ('core', 'zb'), pairs)  21 us
    all_to_all x1, blocking collectives, body(): out = lax.all_to_all(out, ('layer', 'zc'), 0, 0, tiled=True)  15.1 us
    ppermute x3, starting transfers between devices, body(): lax.ppermute(mine, 'x', [(i, (i - k) % nx) for i in range(nx)])  13.7 us
    pallas_call x2, Pallas kernels, product(): pl.pallas_call(functools.partial(product_kernel, parts=parts, brows=brows...  7.91 us
    unnamed x12, local copies, waits for them, and re-layouts  4.07 us
    ppermute x1, starting transfers between devices, body(): far = lax.ppermute(mine, 'zc', [(0, 1), (1, 0)])  3.82 us
  transfers between devices with their start and end apart: 12, of which 5 were waited for; matrix products, arithmetic and copies ran while one was open for 2% of the time, Pallas kernels for 6%

profile of v2, /device:TPU:2, one launch (start us, length us, event | category | flops | bytes accessed | tf_op | source)
XLA Modules:
  0.0 105.6 jit_solution(4434175239489624973)
XLA Ops:
  0.0 3.8 %collective-permute-start.2 = (bf16[1024,128]{1,0:T(8,128)(2,1)}, bf16[1024,128]{1,0:T(8,128)(2,1)S(1)}, u32[]{:S(2)}, u32[]{:S(2)}) collective-permute-start(bf16[1024,128]{1,0:T(8,128)(2,1)} %bitcast.24), channel_id=1, source_target_pairs={{0,1},{1,0},{2,3},{3,2},{4,5},{5,4},{6,7},{7,6},{8,9},{9,8},{10,11... | collective-permute-start | bytes 786440 | tf_op jit(solution)/shard_map/ppermute | solution.py:186
  3.8 1.7 %pack.1.refs_2_ = bf16[16,8320]{1,0:T(8,128)(2,1)} custom-call(bf16[2,16,4096]{2,1,0:T(8,128)(2,1)} %bitcast.27, s32[2,16]{1,0:T(2,128)} %bitcast.28, s32[2]{0:T(128)} %bitcast.29), custom_call_target="tpu_custom_call" | custom-call | tf_op jit(solution)/shard_map/pack/pallas_call | solution.py:171
  5.5 5.2 %collective-permute-start = (bf16[16,8320]{1,0:T(8,128)(2,1)}, bf16[16,8320]{1,0:T(8,128)(2,1)S(1)}, u32[]{:S(2)}, u32[]{:S(2)}) collective-permute-start(bf16[16,8320]{1,0:T(8,128)(2,1)} %pack.1.refs_2_), channel_id=1, source_target_pairs={{0,2},{2,4},{4,6},{6,8},{8,10},{10,12},{12,14},{14,0},{16,30},{18,... | collective-permute-start | bytes 798728 | tf_op jit(solution)/shard_map/ppermute | solution.py:169
  10.7 1.0 pad_maximum_fusion
  11.7 8.4 %collective-permute-start.4 = (bf16[2048,128]{1,0:T(8,128)(2,1)S(1)}, bf16[2048,128]{1,0:T(8,128)(2,1)S(1)}, u32[]{:S(2)}, u32[]{:S(2)}) collective-permute-start(bf16[2048,128]{1,0:T(8,128)(2,1)S(1)} %pad_maximum_fusion), channel_id=1, source_target_pairs={{0,96},{32,0},{64,32},{96,64},{1,97},{33,1},{65,33},{97,65},{2,98}... | collective-permute-start | bytes 1572872 | tf_op jit(solution)/shard_map/ppermute | solution.py:190
  20.1 1.9 %collective-permute-start.5 = (bf16[2048,128]{1,0:T(8,128)(2,1)S(1)}, bf16[2048,128]{1,0:T(8,128)(2,1)S(1)}, u32[]{:S(2)}, u32[]{:S(2)}) collective-permute-start(bf16[2048,128]{1,0:T(8,128)(2,1)S(1)} %pad_maximum_fusion), channel_id=1, source_target_pairs={{0,64},{32,96},{64,0},{96,32},{1,65},{33,97},{65,1},{97,33},{2,66}... | collective-permute-start | bytes 1572872 | tf_op jit(solution)/shard_map/ppermute | solution.py:190
  22.1 3.4 %collective-permute-start.6 = (bf16[2048,128]{1,0:T(8,128)(2,1)S(1)}, bf16[2048,128]{1,0:T(8,128)(2,1)S(1)}, u32[]{:S(2)}, u32[]{:S(2)}) collective-permute-start(bf16[2048,128]{1,0:T(8,128)(2,1)S(1)} %pad_maximum_fusion), channel_id=1, source_target_pairs={{0,32},{32,64},{64,96},{96,0},{1,33},{33,65},{65,97},{97,1},{2,34}... | collective-permute-start | bytes 1572872 | tf_op jit(solution)/shard_map/ppermute | solution.py:190
  25.4 8.8 %collective-permute-start.3 = (bf16[16,8320]{1,0:T(8,128)(2,1)}, bf16[16,8320]{1,0:T(8,128)(2,1)S(1)}, u32[]{:S(2)}, u32[]{:S(2)}) collective-permute-start(bf16[16,8320]{1,0:T(8,128)(2,1)} %pack.1.refs_2_), channel_id=1, source_target_pairs={{0,14},{2,0},{4,2},{6,4},{8,6},{10,8},{12,10},{14,12},{16,18},{18,... | collective-permute-start | bytes 798728 | tf_op jit(solution)/shard_map/ppermute | solution.py:169
  34.2 1.9 %collective-permute-start.1 = (bf16[16,8320]{1,0:T(8,128)(2,1)S(1)}, bf16[16,8320]{1,0:T(8,128)(2,1)S(1)}, u32[]{:S(2)}, u32[]{:S(2)}) collective-permute-start(bf16[16,8320]{1,0:T(8,128)(2,1)S(1)} %collective-permute-done.refs_3_), channel_id=1, source_target_pairs={{0,2},{2,4},{4,6},{6,8},{8,10},{10,12},{12,14},{14,0},{16,30},{18,... | collective-permute-start | bytes 798728 | tf_op jit(solution)/shard_map/ppermute | solution.py:169
  37.2 8.6 %collective-permute-done.3.refs_4_ = bf16[16,8320]{1,0:T(8,128)(2,1)S(1)} collective-permute-done((bf16[16,8320]{1,0:T(8,128)(2,1)}, bf16[16,8320]{1,0:T(8,128)(2,1)S(1)}, u32[]{:S(2)}, u32[]{:S(2)}) %collective-permute-start.3) | collective-permute-done | bytes 266272 | tf_op jit(solution)/shard_map/ppermute | solution.py:169
  46.3 2.0 %collective-permute-start.9 = (bf16[8192,128]{1,0:T(8,128)(2,1)S(1)}, bf16[8192,128]{1,0:T(8,128)(2,1)S(1)}, u32[]{:S(2)}, u32[]{:S(2)}) collective-permute-start(bf16[8192,128]{1,0:T(8,128)(2,1)S(1)} %constant_dynamic-update-slice_fusion), channel_id=1, source_target_pairs={{0,16},{16,0},{1,17},{17,1},{2,18},{18,2},{3,19},{19,3},{4,20},{20... | collective-permute-start | bytes 6291464 | tf_op jit(solution)/shard_map/ppermute | solution.py:200
  48.3 6.5 %collective-permute-start.8 = (bf16[16,8320]{1,0:T(8,128)(2,1)S(1)}, bf16[16,8320]{1,0:T(8,128)(2,1)}, u32[]{:S(2)}, u32[]{:S(2)}) collective-permute-start(bf16[16,8320]{1,0:T(8,128)(2,1)S(1)} %collective-permute-done.3.refs_4_), channel_id=1, source_target_pairs={{0,14},{2,0},{4,2},{6,4},{8,6},{10,8},{12,10},{14,12},{16,18},{18,... | collective-permute-start | bytes 798728 | tf_op jit(solution)/shard_map/ppermute | solution.py:169
  54.8 1.9 %collective-permute-start.7 = (bf16[16,8320]{1,0:T(8,128)(2,1)S(1)}, bf16[16,8320]{1,0:T(8,128)(2,1)S(1)}, u32[]{:S(2)}, u32[]{:S(2)}) collective-permute-start(bf16[16,8320]{1,0:T(8,128)(2,1)S(1)} %collective-permute-done.1.refs_5_), channel_id=1, source_target_pairs={{0,2},{2,4},{4,6},{6,8},{8,10},{10,12},{12,14},{14,0},{16,30},{18,... | collective-permute-start | bytes 798728 | tf_op jit(solution)/shard_map/ppermute | solution.py:169
  56.7 8.0 %collective-permute-done.8.refs_6_ = bf16[16,8320]{1,0:T(8,128)(2,1)} collective-permute-done((bf16[16,8320]{1,0:T(8,128)(2,1)S(1)}, bf16[16,8320]{1,0:T(8,128)(2,1)}, u32[]{:S(2)}, u32[]{:S(2)}) %collective-permute-start.8) | collective-permute-done | bytes 266272 | tf_op jit(solution)/shard_map/ppermute | solution.py:169
  64.7 6.8 %collective-permute-start.10 = (bf16[16,8320]{1,0:T(8,128)(2,1)}, bf16[16,8320]{1,0:T(8,128)(2,1)}, u32[]{:S(2)}, u32[]{:S(2)}) collective-permute-start(bf16[16,8320]{1,0:T(8,128)(2,1)} %collective-permute-done.8.refs_6_), channel_id=1, source_target_pairs={{0,14},{2,0},{4,2},{6,4},{8,6},{10,8},{12,10},{14,12},{16,18},{18,... | collective-permute-start | bytes 798728 | tf_op jit(solution)/shard_map/ppermute | solution.py:169
  71.6 1.3 %copy-done = bf16[8192,128]{1,0:T(8,128)(2,1)} copy-done((bf16[8192,128]{1,0:T(8,128)(2,1)}, bf16[8192,128]{1,0:T(8,128)(2,1)S(1)}, u32[]{:S(2)}) %copy-start) | copy-done | bytes 2097176
  72.9 1.9 %collective-permute-start.11 = (bf16[16,8320]{1,0:T(8,128)(2,1)S(1)}, bf16[16,8320]{1,0:T(8,128)(2,1)}, u32[]{:S(2)}, u32[]{:S(2)}) collective-permute-start(bf16[16,8320]{1,0:T(8,128)(2,1)S(1)} %collective-permute-done.7.refs_2_), channel_id=1, source_target_pairs={{0,2},{2,4},{4,6},{6,8},{8,10},{10,12},{12,14},{14,0},{16,30},{18,... | collective-permute-start | bytes 798728 | tf_op jit(solution)/shard_map/ppermute | solution.py:169
  75.2 1.6 %copy-done.1 = bf16[8192,128]{1,0:T(8,128)(2,1)S(1)} copy-done((bf16[8192,128]{1,0:T(8,128)(2,1)S(1)}, bf16[8192,128]{1,0:T(8,128)(2,1)}, u32[]{:S(2)}) %copy-start.1) | copy-done | bytes 2097176
  76.8 4.5 %product.1.refs_7_ = f32[4,256,128]{2,1,0:T(8,128)S(1)} custom-call(s32[2,64]{1,0:T(2,128)S(1)} %bitcast.22, s32[8]{0:T(128)S(1)} %stack.54.refs_1_, bf16[16,8320]{1,0:T(8,128)(2,1)S(1)} %copy-done.2, bf16[16,8320]{1,0:T(8,128)(2,1)S(1)} %collective-permute-done.refs_3_, bf16[16,8320]{1,0:T(8,128)(2,1)S(1)} %collective-permute-done.3.refs_4_, ...), custom_call_target="tpu_custom_call" | custom-call | flops 1342177280 | bytes 8388608 | tf_op jit(solution)/shard_map/product/pallas_call | solution.py:121
  81.3 1.1 collective-permute-done.10.refs_3_
  82.3 3.1 %collective-permute-done.11.refs_4_ = bf16[16,8320]{1,0:T(8,128)(2,1)} collective-permute-done((bf16[16,8320]{1,0:T(8,128)(2,1)S(1)}, bf16[16,8320]{1,0:T(8,128)(2,1)}, u32[]{:S(2)}, u32[]{:S(2)}) %collective-permute-start.11) | collective-permute-done | bytes 266272 | tf_op jit(solution)/shard_map/ppermute | solution.py:169
  85.5 3.4 %product_last.1 = f32[8,64,256]{2,1,0:T(8,128)S(1)} custom-call(s32[2,64]{1,0:T(2,128)S(1)} %bitcast.23, s32[6]{0:T(128)S(1)} %stack.48.refs_1_, bf16[16,8320]{1,0:T(8,128)(2,1)S(1)} %collective-permute-done.7.refs_2_, bf16[16,8320]{1,0:T(8,128)(2,1)} %collective-permute-done.10.refs_3_, bf16[16,8320]{1,0:T(8,128)(2,1)} %collective-permute-done.11.refs_4_, ...), custom_call_target="tpu_custom_call" | custom-call | flops 805306368 | bytes 8388608 | tf_op jit(solution)/shard_map/product_last/pallas_call | solution.py:121
  88.9 15.1 %all_to_all.5.parts_ref = f32[8,64,256]{2,1,0:T(8,128)} all-to-all(f32[8,64,256]{2,1,0:T(8,128)S(1)} %product_last.1), channel_id=1, replica_groups=mesh['layer'=4,'x'=4,'core'=2,'zb'=8,'zc'=2] {'layer','zc'}, dimensions={0} | all-to-all | bytes 1048576 | tf_op jit(solution)/shard_map/all_to_all | solution.py:223
  103.9 1.7 %finish.1 = bf16[128,128]{1,0:T(8,128)(2,1)} custom-call(f32[8,64,256]{2,1,0:T(8,128)} %all_to_all.5.parts_ref), custom_call_target="tpu_custom_call" | custom-call | tf_op jit(solution)/shard_map/finish/pallas_call | solution.py:224
  (21 shorter events, 1.7 us)
Async XLA Ops:
  0.0 10.7 %collective-permute-start.2 = (bf16[1024,128]{1,0:T(8,128)(2,1)}, bf16[1024,128]{1,0:T(8,128)(2,1)S(1)}, u32[]{:S(2)}, u32[]{:S(2)}) collective-permute-start(bf16[1024,128]{1,0:T(8,128)(2,1)} %bitcast.24), channel_id=1, source_target_pairs={{0,1},{1,0},{2,3},{3,2},{4,5},{5,4},{6,7},{7,6},{8,9},{9,8},{10,11... | collective-permute-start | bytes 786440 | tf_op jit(solution)/shard_map/ppermute | solution.py:186
  5.5 28.7 %collective-permute-start = (bf16[16,8320]{1,0:T(8,128)(2,1)}, bf16[16,8320]{1,0:T(8,128)(2,1)S(1)}, u32[]{:S(2)}, u32[]{:S(2)}) collective-permute-start(bf16[16,8320]{1,0:T(8,128)(2,1)} %pack.1.refs_2_), channel_id=1, source_target_pairs={{0,2},{2,4},{4,6},{6,8},{8,10},{10,12},{12,14},{14,0},{16,30},{18,... | collective-permute-start | bytes 798728 | tf_op jit(solution)/shard_map/ppermute | solution.py:169
  11.7 34.3 %collective-permute-start.4 = (bf16[2048,128]{1,0:T(8,128)(2,1)S(1)}, bf16[2048,128]{1,0:T(8,128)(2,1)S(1)}, u32[]{:S(2)}, u32[]{:S(2)}) collective-permute-start(bf16[2048,128]{1,0:T(8,128)(2,1)S(1)} %pad_maximum_fusion), channel_id=1, source_target_pairs={{0,96},{32,0},{64,32},{96,64},{1,97},{33,1},{65,33},{97,65},{2,98}... | collective-permute-start | bytes 1572872 | tf_op jit(solution)/shard_map/ppermute | solution.py:190
  20.1 25.9 %collective-permute-start.5 = (bf16[2048,128]{1,0:T(8,128)(2,1)S(1)}, bf16[2048,128]{1,0:T(8,128)(2,1)S(1)}, u32[]{:S(2)}, u32[]{:S(2)}) collective-permute-start(bf16[2048,128]{1,0:T(8,128)(2,1)S(1)} %pad_maximum_fusion), channel_id=1, source_target_pairs={{0,64},{32,96},{64,0},{96,32},{1,65},{33,97},{65,1},{97,33},{2,66}... | collective-permute-start | bytes 1572872 | tf_op jit(solution)/shard_map/ppermute | solution.py:190
  22.1 24.0 %collective-permute-start.6 = (bf16[2048,128]{1,0:T(8,128)(2,1)S(1)}, bf16[2048,128]{1,0:T(8,128)(2,1)S(1)}, u32[]{:S(2)}, u32[]{:S(2)}) collective-permute-start(bf16[2048,128]{1,0:T(8,128)(2,1)S(1)} %pad_maximum_fusion), channel_id=1, source_target_pairs={{0,32},{32,64},{64,96},{96,0},{1,33},{33,65},{65,97},{97,1},{2,34}... | collective-permute-start | bytes 1572872 | tf_op jit(solution)/shard_map/ppermute | solution.py:190
  25.4 20.3 %collective-permute-start.3 = (bf16[16,8320]{1,0:T(8,128)(2,1)}, bf16[16,8320]{1,0:T(8,128)(2,1)S(1)}, u32[]{:S(2)}, u32[]{:S(2)}) collective-permute-start(bf16[16,8320]{1,0:T(8,128)(2,1)} %pack.1.refs_2_), channel_id=1, source_target_pairs={{0,14},{2,0},{4,2},{6,4},{8,6},{10,8},{12,10},{14,12},{16,18},{18,... | collective-permute-start | bytes 798728 | tf_op jit(solution)/shard_map/ppermute | solution.py:169
  34.2 11.8 %collective-permute-start.1 = (bf16[16,8320]{1,0:T(8,128)(2,1)S(1)}, bf16[16,8320]{1,0:T(8,128)(2,1)S(1)}, u32[]{:S(2)}, u32[]{:S(2)}) collective-permute-start(bf16[16,8320]{1,0:T(8,128)(2,1)S(1)} %collective-permute-done.refs_3_), channel_id=1, source_target_pairs={{0,2},{2,4},{4,6},{6,8},{8,10},{10,12},{12,14},{14,0},{16,30},{18,... | collective-permute-start | bytes 798728 | tf_op jit(solution)/shard_map/ppermute | solution.py:169
  37.2 38.0 %copy-start.2 = (bf16[16,8320]{1,0:T(8,128)(2,1)S(1)}, bf16[16,8320]{1,0:T(8,128)(2,1)}, u32[]{:S(2)}) copy-start(bf16[16,8320]{1,0:T(8,128)(2,1)} %pack.1.refs_2_) | copy-start | bytes 798724
  37.2 38.0 %copy-start.3 = (s32[1,2,64]{2,1,0:T(2,128)S(1)}, s32[1,2,64]{2,1,0:T(2,128)}, u32[]{:S(2)}) copy-start(s32[1,2,64]{2,1,0:T(2,128)} %param.9) | copy-start | bytes 1540
  46.3 25.3 %collective-permute-start.9 = (bf16[8192,128]{1,0:T(8,128)(2,1)S(1)}, bf16[8192,128]{1,0:T(8,128)(2,1)S(1)}, u32[]{:S(2)}, u32[]{:S(2)}) collective-permute-start(bf16[8192,128]{1,0:T(8,128)(2,1)S(1)} %constant_dynamic-update-slice_fusion), channel_id=1, source_target_pairs={{0,16},{16,0},{1,17},{17,1},{2,18},{18,2},{3,19},{19,3},{4,20},{20... | collective-permute-start | bytes 6291464 | tf_op jit(solution)/shard_map/ppermute | solution.py:200
  48.3 16.4 %collective-permute-start.8 = (bf16[16,8320]{1,0:T(8,128)(2,1)S(1)}, bf16[16,8320]{1,0:T(8,128)(2,1)}, u32[]{:S(2)}, u32[]{:S(2)}) collective-permute-start(bf16[16,8320]{1,0:T(8,128)(2,1)S(1)} %collective-permute-done.3.refs_4_), channel_id=1, source_target_pairs={{0,14},{2,0},{4,2},{6,4},{8,6},{10,8},{12,10},{14,12},{16,18},{18,... | collective-permute-start | bytes 798728 | tf_op jit(solution)/shard_map/ppermute | solution.py:169
  54.8 16.8 %collective-permute-start.7 = (bf16[16,8320]{1,0:T(8,128)(2,1)S(1)}, bf16[16,8320]{1,0:T(8,128)(2,1)S(1)}, u32[]{:S(2)}, u32[]{:S(2)}) collective-permute-start(bf16[16,8320]{1,0:T(8,128)(2,1)S(1)} %collective-permute-done.1.refs_5_), channel_id=1, source_target_pairs={{0,2},{2,4},{4,6},{6,8},{8,10},{10,12},{12,14},{14,0},{16,30},{18,... | collective-permute-start | bytes 798728 | tf_op jit(solution)/shard_map/ppermute | solution.py:169
  64.7 17.6 %collective-permute-start.10 = (bf16[16,8320]{1,0:T(8,128)(2,1)}, bf16[16,8320]{1,0:T(8,128)(2,1)}, u32[]{:S(2)}, u32[]{:S(2)}) collective-permute-start(bf16[16,8320]{1,0:T(8,128)(2,1)} %collective-permute-done.8.refs_6_), channel_id=1, source_target_pairs={{0,14},{2,0},{4,2},{6,4},{8,6},{10,8},{12,10},{14,12},{16,18},{18,... | collective-permute-start | bytes 798728 | tf_op jit(solution)/shard_map/ppermute | solution.py:169
  71.6 1.3 %copy-start = (bf16[8192,128]{1,0:T(8,128)(2,1)}, bf16[8192,128]{1,0:T(8,128)(2,1)S(1)}, u32[]{:S(2)}) copy-start(bf16[8192,128]{1,0:T(8,128)(2,1)S(1)} %collective-permute-done.9) | copy-start | bytes 6291460
  72.9 12.5 %collective-permute-start.11 = (bf16[16,8320]{1,0:T(8,128)(2,1)S(1)}, bf16[16,8320]{1,0:T(8,128)(2,1)}, u32[]{:S(2)}, u32[]{:S(2)}) collective-permute-start(bf16[16,8320]{1,0:T(8,128)(2,1)S(1)} %collective-permute-done.7.refs_2_), channel_id=1, source_target_pairs={{0,2},{2,4},{4,6},{6,8},{8,10},{10,12},{12,14},{14,0},{16,30},{18,... | collective-permute-start | bytes 798728 | tf_op jit(solution)/shard_map/ppermute | solution.py:169
  75.2 1.6 %copy-start.1 = (bf16[8192,128]{1,0:T(8,128)(2,1)S(1)}, bf16[8192,128]{1,0:T(8,128)(2,1)}, u32[]{:S(2)}) copy-start(bf16[8192,128]{1,0:T(8,128)(2,1)} %copy-done) | copy-start | bytes 6291460

commit v3 on v2

--- a/solution.py
+++ b/solution.py
@@ -185,16 +185,16 @@
     mine = modes.reshape(STEPS * depth, width)
     far = lax.ppermute(mine, "zc", [(0, 1), (1, 0)])
     fwd.append(turn(fwd[0], 1))
-    back[0], far = after(back[0], far)
+    back.append(turn(back[0], -1))
+    fwd[1], far = after(fwd[1], far)
+    fwd.append(turn(fwd[1], 1))
     mine = jnp.concatenate([mine, far], axis=0)
     moved = [lax.ppermute(mine, "x", [(i, (i - k) % nx) for i in range(nx)]) for k in range(1, nx)]
-    back.append(turn(back[0], -1))
-    fwd.append(turn(fwd[1], 1))
     back[1], fwd[1] = after(back[1], fwd[1])
     back.append(turn(back[1], -1))
-    fwd[2], back[1], *moved = after(fwd[2], back[1], *moved)
+    fwd[2], back[1] = after(fwd[2], back[1])
     fwd.append(turn(fwd[2], 1))
-    back[2], fwd[2] = after(back[2], fwd[2])
+    back[2], fwd[2], *moved = after(back[2], fwd[2], *moved)
     back.append(turn(back[2], -1))
     mine = jnp.concatenate([mine] + moved, axis=0)
     other = lax.ppermute(mine, "core", [(0, 1), (1, 0)])

time: 106 us -> 114 us (1.075)
  the two profiles are of different devices: /device:TPU:2 before, /device:TPU:1 now
where the time goes in v3:
time: 114 us
  starting transfers between devices  54.1 us (47%)
  waiting for transfers between devices  29.4 us (26%)
  blocking collectives  13.7 us (12%)
  Pallas kernels  11 us (10%)
  local copies, waits for them, and re-layouts  4.32 us (4%)
    ppermute x7, starting transfers between devices, turn(): return lax.ppermute(v, ('core', 'zb'), pairs)  42.2 us
    ppermute x7, waiting for transfers between devices, turn(): return lax.ppermute(v, ('core', 'zb'), pairs)  18.1 us
    all_to_all x1, blocking collectives, body(): out = lax.all_to_all(out, ('layer', 'zc'), 0, 0, tiled=True)  13.7 us
    ppermute x1, waiting for transfers between devices, body(): far = lax.ppermute(mine, 'zc', [(0, 1), (1, 0)])  11.3 us
    pallas_call x2, Pallas kernels, product(): pl.pallas_call(functools.partial(product_kernel, parts=parts, brows=brows...  7.56 us
    ppermute x3, starting transfers between devices, body(): lax.ppermute(mine, 'x', [(i, (i - k) % nx) for i in range(nx)])  7.33 us
    unnamed x12, local copies, waits for them, and re-layouts  4.08 us
    ppermute x1, starting transfers between devices, body(): far = lax.ppermute(mine, 'zc', [(0, 1), (1, 0)])  2.65 us
  transfers between devices with their start and end apart: 12, of which 4 were waited for; matrix products, arithmetic and copies ran while one was open for 2% of the time, Pallas kernels for 4%

profile of v3, /device:TPU:1, one launch (start us, length us, event | category | flops | bytes accessed | tf_op | source)
XLA Modules:
  0.0 113.8 jit_solution(11704808830427515147)
XLA Ops:
  0.0 1.7 %pack.1.refs_2_ = bf16[16,8320]{1,0:T(8,128)(2,1)} custom-call(bf16[2,16,4096]{2,1,0:T(8,128)(2,1)} %bitcast.27, s32[2,16]{1,0:T(2,128)} %bitcast.28, s32[2]{0:T(128)} %bitcast.29), custom_call_target="tpu_custom_call" | custom-call | tf_op jit(solution)/shard_map/pack/pallas_call | solution.py:171
  1.7 12.4 %collective-permute-start = (bf16[16,8320]{1,0:T(8,128)(2,1)}, bf16[16,8320]{1,0:T(8,128)(2,1)S(1)}, u32[]{:S(2)}, u32[]{:S(2)}) collective-permute-start(bf16[16,8320]{1,0:T(8,128)(2,1)} %pack.1.refs_2_), channel_id=1, source_target_pairs={{0,2},{2,4},{4,6},{6,8},{8,10},{10,12},{12,14},{14,0},{16,30},{18,... | collective-permute-start | bytes 798728 | tf_op jit(solution)/shard_map/ppermute | solution.py:169
  14.1 2.6 %collective-permute-start.1 = (bf16[1024,128]{1,0:T(8,128)(2,1)}, bf16[1024,128]{1,0:T(8,128)(2,1)S(1)}, u32[]{:S(2)}, u32[]{:S(2)}) collective-permute-start(bf16[1024,128]{1,0:T(8,128)(2,1)} %bitcast.24), channel_id=1, source_target_pairs={{0,1},{1,0},{2,3},{3,2},{4,5},{5,4},{6,7},{7,6},{8,9},{9,8},{10,11... | collective-permute-start | bytes 786440 | tf_op jit(solution)/shard_map/ppermute | solution.py:186
  16.8 1.9 %collective-permute-start.3 = (bf16[16,8320]{1,0:T(8,128)(2,1)}, bf16[16,8320]{1,0:T(8,128)(2,1)S(1)}, u32[]{:S(2)}, u32[]{:S(2)}) collective-permute-start(bf16[16,8320]{1,0:T(8,128)(2,1)} %pack.1.refs_2_), channel_id=1, source_target_pairs={{0,14},{2,0},{4,2},{6,4},{8,6},{10,8},{12,10},{14,12},{16,18},{18,... | collective-permute-start | bytes 798728 | tf_op jit(solution)/shard_map/ppermute | solution.py:169
  18.7 11.3 %collective-permute-done.1 = bf16[1024,128]{1,0:T(8,128)(2,1)S(1)} collective-permute-done((bf16[1024,128]{1,0:T(8,128)(2,1)}, bf16[1024,128]{1,0:T(8,128)(2,1)S(1)}, u32[]{:S(2)}, u32[]{:S(2)}) %collective-permute-start.1) | collective-permute-done | bytes 262176 | tf_op jit(solution)/shard_map/ppermute | solution.py:186
  30.0 1.0 pad_maximum_fusion
  31.0 2.4 %collective-permute-start.6 = (bf16[2048,128]{1,0:T(8,128)(2,1)S(1)}, bf16[2048,128]{1,0:T(8,128)(2,1)S(1)}, u32[]{:S(2)}, u32[]{:S(2)}) collective-permute-start(bf16[2048,128]{1,0:T(8,128)(2,1)S(1)} %pad_maximum_fusion), channel_id=1, source_target_pairs={{0,96},{32,0},{64,32},{96,64},{1,97},{33,1},{65,33},{97,65},{2,98}... | collective-permute-start | bytes 1572872 | tf_op jit(solution)/shard_map/ppermute | solution.py:192
  33.4 2.4 %collective-permute-start.7 = (bf16[2048,128]{1,0:T(8,128)(2,1)S(1)}, bf16[2048,128]{1,0:T(8,128)(2,1)S(1)}, u32[]{:S(2)}, u32[]{:S(2)}) collective-permute-start(bf16[2048,128]{1,0:T(8,128)(2,1)S(1)} %pad_maximum_fusion), channel_id=1, source_target_pairs={{0,64},{32,96},{64,0},{96,32},{1,65},{33,97},{65,1},{97,33},{2,66}... | collective-permute-start | bytes 1572872 | tf_op jit(solution)/shard_map/ppermute | solution.py:192
  35.8 2.5 %collective-permute-start.8 = (bf16[2048,128]{1,0:T(8,128)(2,1)S(1)}, bf16[2048,128]{1,0:T(8,128)(2,1)S(1)}, u32[]{:S(2)}, u32[]{:S(2)}) collective-permute-start(bf16[2048,128]{1,0:T(8,128)(2,1)S(1)} %pad_maximum_fusion), channel_id=1, source_target_pairs={{0,32},{32,64},{64,96},{96,0},{1,33},{33,65},{65,97},{97,1},{2,34}... | collective-permute-start | bytes 1572872 | tf_op jit(solution)/shard_map/ppermute | solution.py:192
  38.3 6.3 %collective-permute-start.2 = (bf16[16,8320]{1,0:T(8,128)(2,1)S(1)}, bf16[16,8320]{1,0:T(8,128)(2,1)S(1)}, u32[]{:S(2)}, u32[]{:S(2)}) collective-permute-start(bf16[16,8320]{1,0:T(8,128)(2,1)S(1)} %collective-permute-done.refs_3_), channel_id=1, source_target_pairs={{0,2},{2,4},{4,6},{6,8},{8,10},{10,12},{12,14},{14,0},{16,30},{18,... | collective-permute-start | bytes 798728 | tf_op jit(solution)/shard_map/ppermute | solution.py:169
  44.6 1.9 %collective-permute-start.5 = (bf16[16,8320]{1,0:T(8,128)(2,1)S(1)}, bf16[16,8320]{1,0:T(8,128)(2,1)S(1)}, u32[]{:S(2)}, u32[]{:S(2)}) collective-permute-start(bf16[16,8320]{1,0:T(8,128)(2,1)S(1)} %collective-permute-done.3.refs_4_), channel_id=1, source_target_pairs={{0,14},{2,0},{4,2},{6,4},{8,6},{10,8},{12,10},{14,12},{16,18},{18,... | collective-permute-start | bytes 798728 | tf_op jit(solution)/shard_map/ppermute | solution.py:169
  47.6 2.5 %collective-permute-done.2.refs_5_ = bf16[16,8320]{1,0:T(8,128)(2,1)S(1)} collective-permute-done((bf16[16,8320]{1,0:T(8,128)(2,1)S(1)}, bf16[16,8320]{1,0:T(8,128)(2,1)S(1)}, u32[]{:S(2)}, u32[]{:S(2)}) %collective-permute-start.2) | collective-permute-done | bytes 266272 | tf_op jit(solution)/shard_map/ppermute | solution.py:169
  50.1 6.6 %collective-permute-done.5.refs_6_ = bf16[16,8320]{1,0:T(8,128)(2,1)S(1)} collective-permute-done((bf16[16,8320]{1,0:T(8,128)(2,1)S(1)}, bf16[16,8320]{1,0:T(8,128)(2,1)S(1)}, u32[]{:S(2)}, u32[]{:S(2)}) %collective-permute-start.5) | collective-permute-done | bytes 266272 | tf_op jit(solution)/shard_map/ppermute | solution.py:169
  56.9 1.9 %collective-permute-start.9 = (bf16[8192,128]{1,0:T(8,128)(2,1)S(1)}, bf16[8192,128]{1,0:T(8,128)(2,1)S(1)}, u32[]{:S(2)}, u32[]{:S(2)}) collective-permute-start(bf16[8192,128]{1,0:T(8,128)(2,1)S(1)} %constant_dynamic-update-slice_fusion), channel_id=1, source_target_pairs={{0,16},{16,0},{1,17},{17,1},{2,18},{18,2},{3,19},{19,3},{4,20},{20... | collective-permute-start | bytes 6291464 | tf_op jit(solution)/shard_map/ppermute | solution.py:200
  58.8 11.4 %collective-permute-start.4 = (bf16[16,8320]{1,0:T(8,128)(2,1)S(1)}, bf16[16,8320]{1,0:T(8,128)(2,1)}, u32[]{:S(2)}, u32[]{:S(2)}) collective-permute-start(bf16[16,8320]{1,0:T(8,128)(2,1)S(1)} %collective-permute-done.2.refs_5_), channel_id=1, source_target_pairs={{0,2},{2,4},{4,6},{6,8},{8,10},{10,12},{12,14},{14,0},{16,30},{18,... | collective-permute-start | bytes 798728 | tf_op jit(solution)/shard_map/ppermute | solution.py:169
  70.3 1.9 %collective-permute-start.10 = (bf16[16,8320]{1,0:T(8,128)(2,1)S(1)}, bf16[16,8320]{1,0:T(8,128)(2,1)}, u32[]{:S(2)}, u32[]{:S(2)}) collective-permute-start(bf16[16,8320]{1,0:T(8,128)(2,1)S(1)} %collective-permute-done.5.refs_6_), channel_id=1, source_target_pairs={{0,14},{2,0},{4,2},{6,4},{8,6},{10,8},{12,10},{14,12},{16,18},{18,... | collective-permute-start | bytes 798728 | tf_op jit(solution)/shard_map/ppermute | solution.py:169
  72.2 9.0 %collective-permute-done.4.refs_2_ = bf16[16,8320]{1,0:T(8,128)(2,1)} collective-permute-done((bf16[16,8320]{1,0:T(8,128)(2,1)S(1)}, bf16[16,8320]{1,0:T(8,128)(2,1)}, u32[]{:S(2)}, u32[]{:S(2)}) %collective-permute-start.4) | collective-permute-done | bytes 266272 | tf_op jit(solution)/shard_map/ppermute | solution.py:169
  81.2 1.3 %copy-done = bf16[8192,128]{1,0:T(8,128)(2,1)} copy-done((bf16[8192,128]{1,0:T(8,128)(2,1)}, bf16[8192,128]{1,0:T(8,128)(2,1)S(1)}, u32[]{:S(2)}) %copy-start) | copy-done | bytes 2097176
  82.6 6.3 %collective-permute-start.11 = (bf16[16,8320]{1,0:T(8,128)(2,1)}, bf16[16,8320]{1,0:T(8,128)(2,1)}, u32[]{:S(2)}, u32[]{:S(2)}) collective-permute-start(bf16[16,8320]{1,0:T(8,128)(2,1)} %collective-permute-done.4.refs_2_), channel_id=1, source_target_pairs={{0,2},{2,4},{4,6},{6,8},{8,10},{10,12},{12,14},{14,0},{16,30},{18,... | collective-permute-start | bytes 798728 | tf_op jit(solution)/shard_map/ppermute | solution.py:169
  89.2 1.6 %copy-done.1 = bf16[8192,128]{1,0:T(8,128)(2,1)S(1)} copy-done((bf16[8192,128]{1,0:T(8,128)(2,1)S(1)}, bf16[8192,128]{1,0:T(8,128)(2,1)}, u32[]{:S(2)}) %copy-start.1) | copy-done | bytes 2097176
  90.8 4.1 %product.1.refs_7_ = f32[4,256,128]{2,1,0:T(8,128)S(1)} custom-call(s32[2,64]{1,0:T(2,128)S(1)} %bitcast.22, s32[8]{0:T(128)S(1)} %stack.54.refs_1_, bf16[16,8320]{1,0:T(8,128)(2,1)S(1)} %copy-done.2, bf16[16,8320]{1,0:T(8,128)(2,1)S(1)} %collective-permute-done.refs_3_, bf16[16,8320]{1,0:T(8,128)(2,1)S(1)} %collective-permute-done.3.refs_4_, ...), custom_call_target="tpu_custom_call" | custom-call | flops 1342177280 | bytes 8388608 | tf_op jit(solution)/shard_map/product/pallas_call | solution.py:121
  94.9 3.5 %product_last.1 = f32[8,64,256]{2,1,0:T(8,128)S(1)} custom-call(s32[2,64]{1,0:T(2,128)S(1)} %bitcast.23, s32[6]{0:T(128)S(1)} %stack.48.refs_1_, bf16[16,8320]{1,0:T(8,128)(2,1)} %collective-permute-done.4.refs_2_, bf16[16,8320]{1,0:T(8,128)(2,1)} %collective-permute-done.10.refs_3_, bf16[16,8320]{1,0:T(8,128)(2,1)} %collective-permute-done.11.refs_4_, ...), custom_call_target="tpu_custom_call" | custom-call | flops 805306368 | bytes 8388608 | tf_op jit(solution)/shard_map/product_last/pallas_call | solution.py:121
  98.4 13.7 %all_to_all.5.parts_ref = f32[8,64,256]{2,1,0:T(8,128)} all-to-all(f32[8,64,256]{2,1,0:T(8,128)S(1)} %product_last.1), channel_id=1, replica_groups=mesh['layer'=4,'x'=4,'core'=2,'zb'=8,'zc'=2] {'layer','zc'}, dimensions={0} | all-to-all | bytes 1048576 | tf_op jit(solution)/shard_map/all_to_all | solution.py:223
  112.2 1.7 %finish.1 = bf16[128,128]{1,0:T(8,128)(2,1)} custom-call(f32[8,64,256]{2,1,0:T(8,128)} %all_to_all.5.parts_ref), custom_call_target="tpu_custom_call" | custom-call | tf_op jit(solution)/shard_map/finish/pallas_call | solution.py:224
  (21 shorter events, 1.4 us)
Async XLA Ops:
  1.7 28.3 %collective-permute-start = (bf16[16,8320]{1,0:T(8,128)(2,1)}, bf16[16,8320]{1,0:T(8,128)(2,1)S(1)}, u32[]{:S(2)}, u32[]{:S(2)}) collective-permute-start(bf16[16,8320]{1,0:T(8,128)(2,1)} %pack.1.refs_2_), channel_id=1, source_target_pairs={{0,2},{2,4},{4,6},{6,8},{8,10},{10,12},{12,14},{14,0},{16,30},{18,... | collective-permute-start | bytes 798728 | tf_op jit(solution)/shard_map/ppermute | solution.py:169
  14.1 15.9 %collective-permute-start.1 = (bf16[1024,128]{1,0:T(8,128)(2,1)}, bf16[1024,128]{1,0:T(8,128)(2,1)S(1)}, u32[]{:S(2)}, u32[]{:S(2)}) collective-permute-start(bf16[1024,128]{1,0:T(8,128)(2,1)} %bitcast.24), channel_id=1, source_target_pairs={{0,1},{1,0},{2,3},{3,2},{4,5},{5,4},{6,7},{7,6},{8,9},{9,8},{10,11... | collective-permute-start | bytes 786440 | tf_op jit(solution)/shard_map/ppermute | solution.py:186
  16.8 27.8 %collective-permute-start.3 = (bf16[16,8320]{1,0:T(8,128)(2,1)}, bf16[16,8320]{1,0:T(8,128)(2,1)S(1)}, u32[]{:S(2)}, u32[]{:S(2)}) collective-permute-start(bf16[16,8320]{1,0:T(8,128)(2,1)} %pack.1.refs_2_), channel_id=1, source_target_pairs={{0,14},{2,0},{4,2},{6,4},{8,6},{10,8},{12,10},{14,12},{16,18},{18,... | collective-permute-start | bytes 798728 | tf_op jit(solution)/shard_map/ppermute | solution.py:169
  31.0 25.7 %collective-permute-start.6 = (bf16[2048,128]{1,0:T(8,128)(2,1)S(1)}, bf16[2048,128]{1,0:T(8,128)(2,1)S(1)}, u32[]{:S(2)}, u32[]{:S(2)}) collective-permute-start(bf16[2048,128]{1,0:T(8,128)(2,1)S(1)} %pad_maximum_fusion), channel_id=1, source_target_pairs={{0,96},{32,0},{64,32},{96,64},{1,97},{33,1},{65,33},{97,65},{2,98}... | collective-permute-start | bytes 1572872 | tf_op jit(solution)/shard_map/ppermute | solution.py:192
  33.4 23.3 %collective-permute-start.7 = (bf16[2048,128]{1,0:T(8,128)(2,1)S(1)}, bf16[2048,128]{1,0:T(8,128)(2,1)S(1)}, u32[]{:S(2)}, u32[]{:S(2)}) collective-permute-start(bf16[2048,128]{1,0:T(8,128)(2,1)S(1)} %pad_maximum_fusion), channel_id=1, source_target_pairs={{0,64},{32,96},{64,0},{96,32},{1,65},{33,97},{65,1},{97,33},{2,66}... | collective-permute-start | bytes 1572872 | tf_op jit(solution)/shard_map/ppermute | solution.py:192
  35.8 20.9 %collective-permute-start.8 = (bf16[2048,128]{1,0:T(8,128)(2,1)S(1)}, bf16[2048,128]{1,0:T(8,128)(2,1)S(1)}, u32[]{:S(2)}, u32[]{:S(2)}) collective-permute-start(bf16[2048,128]{1,0:T(8,128)(2,1)S(1)} %pad_maximum_fusion), channel_id=1, source_target_pairs={{0,32},{32,64},{64,96},{96,0},{1,33},{33,65},{65,97},{97,1},{2,34}... | collective-permute-start | bytes 1572872 | tf_op jit(solution)/shard_map/ppermute | solution.py:192
  38.3 11.8 %collective-permute-start.2 = (bf16[16,8320]{1,0:T(8,128)(2,1)S(1)}, bf16[16,8320]{1,0:T(8,128)(2,1)S(1)}, u32[]{:S(2)}, u32[]{:S(2)}) collective-permute-start(bf16[16,8320]{1,0:T(8,128)(2,1)S(1)} %collective-permute-done.refs_3_), channel_id=1, source_target_pairs={{0,2},{2,4},{4,6},{6,8},{8,10},{10,12},{12,14},{14,0},{16,30},{18,... | collective-permute-start | bytes 798728 | tf_op jit(solution)/shard_map/ppermute | solution.py:169
  44.6 12.0 %collective-permute-start.5 = (bf16[16,8320]{1,0:T(8,128)(2,1)S(1)}, bf16[16,8320]{1,0:T(8,128)(2,1)S(1)}, u32[]{:S(2)}, u32[]{:S(2)}) collective-permute-start(bf16[16,8320]{1,0:T(8,128)(2,1)S(1)} %collective-permute-done.3.refs_4_), channel_id=1, source_target_pairs={{0,14},{2,0},{4,2},{6,4},{8,6},{10,8},{12,10},{14,12},{16,18},{18,... | collective-permute-start | bytes 798728 | tf_op jit(solution)/shard_map/ppermute | solution.py:169
  47.5 41.7 %copy-start.2 = (bf16[16,8320]{1,0:T(8,128)(2,1)S(1)}, bf16[16,8320]{1,0:T(8,128)(2,1)}, u32[]{:S(2)}) copy-start(bf16[16,8320]{1,0:T(8,128)(2,1)} %pack.1.refs_2_) | copy-start | bytes 798724
  47.5 41.7 %copy-start.3 = (s32[1,2,64]{2,1,0:T(2,128)S(1)}, s32[1,2,64]{2,1,0:T(2,128)}, u32[]{:S(2)}) copy-start(s32[1,2,64]{2,1,0:T(2,128)} %param.9) | copy-start | bytes 1540
  56.9 24.4 %collective-permute-start.9 = (bf16[8192,128]{1,0:T(8,128)(2,1)S(1)}, bf16[8192,128]{1,0:T(8,128)(2,1)S(1)}, u32[]{:S(2)}, u32[]{:S(2)}) collective-permute-start(bf16[8192,128]{1,0:T(8,128)(2,1)S(1)} %constant_dynamic-update-slice_fusion), channel_id=1, source_target_pairs={{0,16},{16,0},{1,17},{17,1},{2,18},{18,2},{3,19},{19,3},{4,20},{20... | collective-permute-start | bytes 6291464 | tf_op jit(solution)/shard_map/ppermute | solution.py:200
  58.8 22.4 %collective-permute-start.4 = (bf16[16,8320]{1,0:T(8,128)(2,1)S(1)}, bf16[16,8320]{1,0:T(8,128)(2,1)}, u32[]{:S(2)}, u32[]{:S(2)}) collective-permute-start(bf16[16,8320]{1,0:T(8,128)(2,1)S(1)} %collective-permute-done.2.refs_5_), channel_id=1, source_target_pairs={{0,2},{2,4},{4,6},{6,8},{8,10},{10,12},{12,14},{14,0},{16,30},{18,... | collective-permute-start | bytes 798728 | tf_op jit(solution)/shard_map/ppermute | solution.py:169
  70.3 24.7 %collective-permute-start.10 = (bf16[16,8320]{1,0:T(8,128)(2,1)S(1)}, bf16[16,8320]{1,0:T(8,128)(2,1)}, u32[]{:S(2)}, u32[]{:S(2)}) collective-permute-start(bf16[16,8320]{1,0:T(8,128)(2,1)S(1)} %collective-permute-done.5.refs_6_), channel_id=1, source_target_pairs={{0,14},{2,0},{4,2},{6,4},{8,6},{10,8},{12,10},{14,12},{16,18},{18,... | collective-permute-start | bytes 798728 | tf_op jit(solution)/shard_map/ppermute | solution.py:169
  81.2 1.3 %copy-start = (bf16[8192,128]{1,0:T(8,128)(2,1)}, bf16[8192,128]{1,0:T(8,128)(2,1)S(1)}, u32[]{:S(2)}) copy-start(bf16[8192,128]{1,0:T(8,128)(2,1)S(1)} %collective-permute-done.9) | copy-start | bytes 6291460
  82.6 12.3 %collective-permute-start.11 = (bf16[16,8320]{1,0:T(8,128)(2,1)}, bf16[16,8320]{1,0:T(8,128)(2,1)}, u32[]{:S(2)}, u32[]{:S(2)}) collective-permute-start(bf16[16,8320]{1,0:T(8,128)(2,1)} %collective-permute-done.4.refs_2_), channel_id=1, source_target_pairs={{0,2},{2,4},{4,6},{6,8},{8,10},{10,12},{12,14},{14,0},{16,30},{18,... | collective-permute-start | bytes 798728 | tf_op jit(solution)/shard_map/ppermute | solution.py:169
  89.2 1.6 %copy-start.1 = (bf16[8192,128]{1,0:T(8,128)(2,1)S(1)}, bf16[8192,128]{1,0:T(8,128)(2,1)}, u32[]{:S(2)}) copy-start(bf16[8192,128]{1,0:T(8,128)(2,1)} %copy-done) | copy-start | bytes 6291460

commit v4 on v2

--- a/solution.py
+++ b/solution.py
@@ -24,18 +24,12 @@
     b_refs, rest = rest[:2], rest[2:]
     if not first:
         acc_in, rest = rest[0], rest[1:]
-    out_ref, stage_ref, hot_ref, lhs_ref, rhs_ref, b_ref, sem = rest[:7]
-    acc_ref = rest[7] if last else out_ref
+    out_ref, stage_ref, hot_ref, lhs_ref, rhs_ref = rest[:5]
+    acc_ref = rest[5] if last else out_ref
     n = len(parts)
     width = KW * LANES
     chunk = group * LANES
-    per_b = b_ref.shape[0] // 2
-
-    copies = [
-        pltpu.make_async_copy(b_refs[e], b_ref.at[pl.ds(e * per_b, per_b)], sem.at[e]) for e in range(2)
-    ]
-    for copy in copies:
-        copy.start()
+
     for i, part in enumerate(parts):
         for s in range(STEPS):
             ref, off = part[s]
@@ -50,8 +44,6 @@
     else:
         acc_ref[...] = acc_in[...]
     x, core = num_ref[n], num_ref[n + 1]
-    for copy in copies:
-        copy.wait()
 
     def one(i, carry):
         g0 = num_ref[i] * KW
@@ -71,8 +63,8 @@
                 side = (row % 2 + core) % 2
                 ahead = (row // 2 + 4 - x) % 4
                 for j in range(group):
-                    at = (((side * 4 + ahead) * group + j) * STEPS + s) * blks + p % blks
-                    blk = b_ref[at]
+                    at = ((ahead * group + j) * STEPS + s) * blks + p % blks
+                    blk = jnp.where(side == 0, b_refs[0][at], b_refs[1][at])
                     for h in range(2):
                         r = s * width + bc * LANES + h * BLK
                         c = h * chunk + j * LANES
@@ -112,8 +104,6 @@
         pltpu.VMEM((n, STEPS, KW * brows, slots), jnp.bfloat16),
         pltpu.VMEM((rows, STEPS * KW * LANES), jnp.bfloat16),
         pltpu.VMEM((STEPS * KW * LANES, 2 * group * LANES), jnp.bfloat16),
-        pltpu.VMEM((2 * b[0].shape[0], BLK, LANES), jnp.bfloat16),
-        pltpu.SemaphoreType.DMA((2,)),
     ]
     if last:
         scratch.append(pltpu.VMEM(sums.shape, jnp.float32))
@@ -122,11 +112,11 @@
         functools.partial(
             product_kernel, parts=parts, brows=brows, slots=slots, blks=blks, group=group, first=first, last=last
         ),
-        in_specs=[smem, smem] + [vmem] * len(pieces) + [pl.BlockSpec(memory_space=pl.ANY)] * 2 + [vmem] * (not first),
+        in_specs=[smem, smem] + [vmem] * (len(pieces) + 2 + (not first)),
         out_specs=vmem,
         scratch_shapes=scratch,
         out_shape=outs if last else sums,
-        compiler_params=pltpu.CompilerParams(vmem_limit_bytes=48 * 1024 * 1024),
+        compiler_params=pltpu.CompilerParams(vmem_limit_bytes=20 * 1024 * 1024),
         cost_estimate=pl.CostEstimate(flops=2 * macs, bytes_accessed=8 << 20, transcendentals=0),
         name="product_last" if last else "product",
     )(own, nums, *pieces, *b, *([] if first else [acc]))

time: 106 us -> 106 us (level)
  no operation moved by 1% of the time
where the time goes in v4:
time: 106 us; the launch traced here: 105 us
  starting transfers between devices  52.5 us (50%)
  waiting for transfers between devices  21.3 us (20%)
  blocking collectives  15.1 us (14%)
  Pallas kernels  10.7 us (10%)
  local copies, waits for them, and re-layouts  4.31 us (4%)
    ppermute x7, starting transfers between devices, turn(): return lax.ppermute(v, ('core', 'zb'), pairs)  33 us
    ppermute x7, waiting for transfers between devices, turn(): return lax.ppermute(v, ('core', 'zb'), pairs)  21.3 us
    all_to_all x1, blocking collectives, body(): out = lax.all_to_all(out, ('layer', 'zc'), 0, 0, tiled=True)  15.1 us
    ppermute x3, starting transfers between devices, body(): lax.ppermute(mine, 'x', [(i, (i - k) % nx) for i in range(nx)])  13.7 us
    pallas_call x2, Pallas kernels, product(): pl.pallas_call(functools.partial(product_kernel, parts=parts, brows=brows...  7.3 us
    unnamed x12, local copies, waits for them, and re-layouts  4.07 us
    ppermute x1, starting transfers between devices, body(): far = lax.ppermute(mine, 'zc', [(0, 1), (1, 0)])  3.82 us
  transfers between devices with their start and end apart: 12, of which 5 were waited for; matrix products, arithmetic and copies ran while one was open for 2% of the time, Pallas kernels for 6%

profile of v4, /device:TPU:2, one launch (start us, length us, event | category | flops | bytes accessed | tf_op | source)
XLA Modules:
  0.0 105.4 jit_solution(6913839861665634025)
XLA Ops:
  0.0 3.8 %collective-permute-start.2 = (bf16[1024,128]{1,0:T(8,128)(2,1)}, bf16[1024,128]{1,0:T(8,128)(2,1)S(1)}, u32[]{:S(2)}, u32[]{:S(2)}) collective-permute-start(bf16[1024,128]{1,0:T(8,128)(2,1)} %bitcast.24), channel_id=1, source_target_pairs={{0,1},{1,0},{2,3},{3,2},{4,5},{5,4},{6,7},{7,6},{8,9},{9,8},{10,11... | collective-permute-start | bytes 786440 | tf_op jit(solution)/shard_map/ppermute | solution.py:176
  3.8 1.7 %pack.1.refs_2_ = bf16[16,8320]{1,0:T(8,128)(2,1)} custom-call(bf16[2,16,4096]{2,1,0:T(8,128)(2,1)} %bitcast.27, s32[2,16]{1,0:T(2,128)} %bitcast.28, s32[2]{0:T(128)} %bitcast.29), custom_call_target="tpu_custom_call" | custom-call | tf_op jit(solution)/shard_map/pack/pallas_call | solution.py:161
  5.5 5.2 %collective-permute-start = (bf16[16,8320]{1,0:T(8,128)(2,1)}, bf16[16,8320]{1,0:T(8,128)(2,1)S(1)}, u32[]{:S(2)}, u32[]{:S(2)}) collective-permute-start(bf16[16,8320]{1,0:T(8,128)(2,1)} %pack.1.refs_2_), channel_id=1, source_target_pairs={{0,2},{2,4},{4,6},{6,8},{8,10},{10,12},{12,14},{14,0},{16,30},{18,... | collective-permute-start | bytes 798728 | tf_op jit(solution)/shard_map/ppermute | solution.py:159
  10.7 1.0 pad_maximum_fusion
  11.7 8.4 %collective-permute-start.4 = (bf16[2048,128]{1,0:T(8,128)(2,1)S(1)}, bf16[2048,128]{1,0:T(8,128)(2,1)S(1)}, u32[]{:S(2)}, u32[]{:S(2)}) collective-permute-start(bf16[2048,128]{1,0:T(8,128)(2,1)S(1)} %pad_maximum_fusion), channel_id=1, source_target_pairs={{0,96},{32,0},{64,32},{96,64},{1,97},{33,1},{65,33},{97,65},{2,98}... | collective-permute-start | bytes 1572872 | tf_op jit(solution)/shard_map/ppermute | solution.py:180
  20.1 1.9 %collective-permute-start.5 = (bf16[2048,128]{1,0:T(8,128)(2,1)S(1)}, bf16[2048,128]{1,0:T(8,128)(2,1)S(1)}, u32[]{:S(2)}, u32[]{:S(2)}) collective-permute-start(bf16[2048,128]{1,0:T(8,128)(2,1)S(1)} %pad_maximum_fusion), channel_id=1, source_target_pairs={{0,64},{32,96},{64,0},{96,32},{1,65},{33,97},{65,1},{97,33},{2,66}... | collective-permute-start | bytes 1572872 | tf_op jit(solution)/shard_map/ppermute | solution.py:180
  22.1 3.4 %collective-permute-start.6 = (bf16[2048,128]{1,0:T(8,128)(2,1)S(1)}, bf16[2048,128]{1,0:T(8,128)(2,1)S(1)}, u32[]{:S(2)}, u32[]{:S(2)}) collective-permute-start(bf16[2048,128]{1,0:T(8,128)(2,1)S(1)} %pad_maximum_fusion), channel_id=1, source_target_pairs={{0,32},{32,64},{64,96},{96,0},{1,33},{33,65},{65,97},{97,1},{2,34}... | collective-permute-start | bytes 1572872 | tf_op jit(solution)/shard_map/ppermute | solution.py:180
  25.4 8.8 %collective-permute-start.3 = (bf16[16,8320]{1,0:T(8,128)(2,1)}, bf16[16,8320]{1,0:T(8,128)(2,1)S(1)}, u32[]{:S(2)}, u32[]{:S(2)}) collective-permute-start(bf16[16,8320]{1,0:T(8,128)(2,1)} %pack.1.refs_2_), channel_id=1, source_target_pairs={{0,14},{2,0},{4,2},{6,4},{8,6},{10,8},{12,10},{14,12},{16,18},{18,... | collective-permute-start | bytes 798728 | tf_op jit(solution)/shard_map/ppermute | solution.py:159
  34.2 1.9 %collective-permute-start.1 = (bf16[16,8320]{1,0:T(8,128)(2,1)S(1)}, bf16[16,8320]{1,0:T(8,128)(2,1)S(1)}, u32[]{:S(2)}, u32[]{:S(2)}) collective-permute-start(bf16[16,8320]{1,0:T(8,128)(2,1)S(1)} %collective-permute-done.refs_3_), channel_id=1, source_target_pairs={{0,2},{2,4},{4,6},{6,8},{8,10},{10,12},{12,14},{14,0},{16,30},{18,... | collective-permute-start | bytes 798728 | tf_op jit(solution)/shard_map/ppermute | solution.py:159
  37.2 8.6 %collective-permute-done.3.refs_4_ = bf16[16,8320]{1,0:T(8,128)(2,1)S(1)} collective-permute-done((bf16[16,8320]{1,0:T(8,128)(2,1)}, bf16[16,8320]{1,0:T(8,128)(2,1)S(1)}, u32[]{:S(2)}, u32[]{:S(2)}) %collective-permute-start.3) | collective-permute-done | bytes 266272 | tf_op jit(solution)/shard_map/ppermute | solution.py:159
  46.3 2.0 %collective-permute-start.9 = (bf16[8192,128]{1,0:T(8,128)(2,1)S(1)}, bf16[8192,128]{1,0:T(8,128)(2,1)S(1)}, u32[]{:S(2)}, u32[]{:S(2)}) collective-permute-start(bf16[8192,128]{1,0:T(8,128)(2,1)S(1)} %constant_dynamic-update-slice_fusion), channel_id=1, source_target_pairs={{0,16},{16,0},{1,17},{17,1},{2,18},{18,2},{3,19},{19,3},{4,20},{20... | collective-permute-start | bytes 6291464 | tf_op jit(solution)/shard_map/ppermute | solution.py:190
  48.3 6.5 %collective-permute-start.8 = (bf16[16,8320]{1,0:T(8,128)(2,1)S(1)}, bf16[16,8320]{1,0:T(8,128)(2,1)}, u32[]{:S(2)}, u32[]{:S(2)}) collective-permute-start(bf16[16,8320]{1,0:T(8,128)(2,1)S(1)} %collective-permute-done.3.refs_4_), channel_id=1, source_target_pairs={{0,14},{2,0},{4,2},{6,4},{8,6},{10,8},{12,10},{14,12},{16,18},{18,... | collective-permute-start | bytes 798728 | tf_op jit(solution)/shard_map/ppermute | solution.py:159
  54.8 1.9 %collective-permute-start.7 = (bf16[16,8320]{1,0:T(8,128)(2,1)S(1)}, bf16[16,8320]{1,0:T(8,128)(2,1)S(1)}, u32[]{:S(2)}, u32[]{:S(2)}) collective-permute-start(bf16[16,8320]{1,0:T(8,128)(2,1)S(1)} %collective-permute-done.1.refs_5_), channel_id=1, source_target_pairs={{0,2},{2,4},{4,6},{6,8},{8,10},{10,12},{12,14},{14,0},{16,30},{18,... | collective-permute-start | bytes 798728 | tf_op jit(solution)/shard_map/ppermute | solution.py:159
  56.7 8.0 %collective-permute-done.8.refs_6_ = bf16[16,8320]{1,0:T(8,128)(2,1)} collective-permute-done((bf16[16,8320]{1,0:T(8,128)(2,1)S(1)}, bf16[16,8320]{1,0:T(8,128)(2,1)}, u32[]{:S(2)}, u32[]{:S(2)}) %collective-permute-start.8) | collective-permute-done | bytes 266272 | tf_op jit(solution)/shard_map/ppermute | solution.py:159
  64.7 6.8 %collective-permute-start.10 = (bf16[16,8320]{1,0:T(8,128)(2,1)}, bf16[16,8320]{1,0:T(8,128)(2,1)}, u32[]{:S(2)}, u32[]{:S(2)}) collective-permute-start(bf16[16,8320]{1,0:T(8,128)(2,1)} %collective-permute-done.8.refs_6_), channel_id=1, source_target_pairs={{0,14},{2,0},{4,2},{6,4},{8,6},{10,8},{12,10},{14,12},{16,18},{18,... | collective-permute-start | bytes 798728 | tf_op jit(solution)/shard_map/ppermute | solution.py:159
  71.6 1.3 %copy-done = bf16[8192,128]{1,0:T(8,128)(2,1)} copy-done((bf16[8192,128]{1,0:T(8,128)(2,1)}, bf16[8192,128]{1,0:T(8,128)(2,1)S(1)}, u32[]{:S(2)}) %copy-start) | copy-done | bytes 2097176
  72.9 1.9 %collective-permute-start.11 = (bf16[16,8320]{1,0:T(8,128)(2,1)S(1)}, bf16[16,8320]{1,0:T(8,128)(2,1)}, u32[]{:S(2)}, u32[]{:S(2)}) collective-permute-start(bf16[16,8320]{1,0:T(8,128)(2,1)S(1)} %collective-permute-done.7.refs_2_), channel_id=1, source_target_pairs={{0,2},{2,4},{4,6},{6,8},{8,10},{10,12},{12,14},{14,0},{16,30},{18,... | collective-permute-start | bytes 798728 | tf_op jit(solution)/shard_map/ppermute | solution.py:159
  75.2 1.6 %copy-done.1 = bf16[8192,128]{1,0:T(8,128)(2,1)S(1)} copy-done((bf16[8192,128]{1,0:T(8,128)(2,1)S(1)}, bf16[8192,128]{1,0:T(8,128)(2,1)}, u32[]{:S(2)}) %copy-start.1) | copy-done | bytes 2097176
  76.8 4.2 %product.1.refs_7_ = f32[4,256,128]{2,1,0:T(8,128)S(1)} custom-call(s32[2,64]{1,0:T(2,128)S(1)} %bitcast.22, s32[8]{0:T(128)S(1)} %stack.54.refs_1_, bf16[16,8320]{1,0:T(8,128)(2,1)S(1)} %copy-done.2, bf16[16,8320]{1,0:T(8,128)(2,1)S(1)} %collective-permute-done.refs_3_, bf16[16,8320]{1,0:T(8,128)(2,1)S(1)} %collective-permute-done.3.refs_4_, ...), custom_call_target="tpu_custom_call" | custom-call | flops 1342177280 | bytes 8388608 | tf_op jit(solution)/shard_map/product/pallas_call | solution.py:111
  81.0 1.4 %collective-permute-done.10.refs_3_ = bf16[16,8320]{1,0:T(8,128)(2,1)} collective-permute-done((bf16[16,8320]{1,0:T(8,128)(2,1)}, bf16[16,8320]{1,0:T(8,128)(2,1)}, u32[]{:S(2)}, u32[]{:S(2)}) %collective-permute-start.10) | collective-permute-done | bytes 266272 | tf_op jit(solution)/shard_map/ppermute | solution.py:159
  82.3 3.1 %collective-permute-done.11.refs_4_ = bf16[16,8320]{1,0:T(8,128)(2,1)} collective-permute-done((bf16[16,8320]{1,0:T(8,128)(2,1)S(1)}, bf16[16,8320]{1,0:T(8,128)(2,1)}, u32[]{:S(2)}, u32[]{:S(2)}) %collective-permute-start.11) | collective-permute-done | bytes 266272 | tf_op jit(solution)/shard_map/ppermute | solution.py:159
  85.5 3.1 %product_last.1 = f32[8,64,256]{2,1,0:T(8,128)S(1)} custom-call(s32[2,64]{1,0:T(2,128)S(1)} %bitcast.23, s32[6]{0:T(128)S(1)} %stack.48.refs_1_, bf16[16,8320]{1,0:T(8,128)(2,1)S(1)} %collective-permute-done.7.refs_2_, bf16[16,8320]{1,0:T(8,128)(2,1)} %collective-permute-done.10.refs_3_, bf16[16,8320]{1,0:T(8,128)(2,1)} %collective-permute-done.11.refs_4_, ...), custom_call_target="tpu_custom_call" | custom-call | flops 805306368 | bytes 8388608 | tf_op jit(solution)/shard_map/product_last/pallas_call | solution.py:111
  88.6 15.1 %all_to_all.5.parts_ref = f32[8,64,256]{2,1,0:T(8,128)} all-to-all(f32[8,64,256]{2,1,0:T(8,128)S(1)} %product_last.1), channel_id=1, replica_groups=mesh['layer'=4,'x'=4,'core'=2,'zb'=8,'zc'=2] {'layer','zc'}, dimensions={0} | all-to-all | bytes 1048576 | tf_op jit(solution)/shard_map/all_to_all | solution.py:213
  103.7 1.7 %finish.1 = bf16[128,128]{1,0:T(8,128)(2,1)} custom-call(f32[8,64,256]{2,1,0:T(8,128)} %all_to_all.5.parts_ref), custom_call_target="tpu_custom_call" | custom-call | tf_op jit(solution)/shard_map/finish/pallas_call | solution.py:214
  (21 shorter events, 1.7 us)
Async XLA Ops:
  0.0 10.7 %collective-permute-start.2 = (bf16[1024,128]{1,0:T(8,128)(2,1)}, bf16[1024,128]{1,0:T(8,128)(2,1)S(1)}, u32[]{:S(2)}, u32[]{:S(2)}) collective-permute-start(bf16[1024,128]{1,0:T(8,128)(2,1)} %bitcast.24), channel_id=1, source_target_pairs={{0,1},{1,0},{2,3},{3,2},{4,5},{5,4},{6,7},{7,6},{8,9},{9,8},{10,11... | collective-permute-start | bytes 786440 | tf_op jit(solution)/shard_map/ppermute | solution.py:176
  5.5 28.7 %collective-permute-start = (bf16[16,8320]{1,0:T(8,128)(2,1)}, bf16[16,8320]{1,0:T(8,128)(2,1)S(1)}, u32[]{:S(2)}, u32[]{:S(2)}) collective-permute-start(bf16[16,8320]{1,0:T(8,128)(2,1)} %pack.1.refs_2_), channel_id=1, source_target_pairs={{0,2},{2,4},{4,6},{6,8},{8,10},{10,12},{12,14},{14,0},{16,30},{18,... | collective-permute-start | bytes 798728 | tf_op jit(solution)/shard_map/ppermute | solution.py:159
  11.7 34.3 %collective-permute-start.4 = (bf16[2048,128]{1,0:T(8,128)(2,1)S(1)}, bf16[2048,128]{1,0:T(8,128)(2,1)S(1)}, u32[]{:S(2)}, u32[]{:S(2)}) collective-permute-start(bf16[2048,128]{1,0:T(8,128)(2,1)S(1)} %pad_maximum_fusion), channel_id=1, source_target_pairs={{0,96},{32,0},{64,32},{96,64},{1,97},{33,1},{65,33},{97,65},{2,98}... | collective-permute-start | bytes 1572872 | tf_op jit(solution)/shard_map/ppermute | solution.py:180
  20.1 25.9 %collective-permute-start.5 = (bf16[2048,128]{1,0:T(8,128)(2,1)S(1)}, bf16[2048,128]{1,0:T(8,128)(2,1)S(1)}, u32[]{:S(2)}, u32[]{:S(2)}) collective-permute-start(bf16[2048,128]{1,0:T(8,128)(2,1)S(1)} %pad_maximum_fusion), channel_id=1, source_target_pairs={{0,64},{32,96},{64,0},{96,32},{1,65},{33,97},{65,1},{97,33},{2,66}... | collective-permute-start | bytes 1572872 | tf_op jit(solution)/shard_map/ppermute | solution.py:180
  22.1 24.0 %collective-permute-start.6 = (bf16[2048,128]{1,0:T(8,128)(2,1)S(1)}, bf16[2048,128]{1,0:T(8,128)(2,1)S(1)}, u32[]{:S(2)}, u32[]{:S(2)}) collective-permute-start(bf16[2048,128]{1,0:T(8,128)(2,1)S(1)} %pad_maximum_fusion), channel_id=1, source_target_pairs={{0,32},{32,64},{64,96},{96,0},{1,33},{33,65},{65,97},{97,1},{2,34}... | collective-permute-start | bytes 1572872 | tf_op jit(solution)/shard_map/ppermute | solution.py:180
  25.4 20.3 %collective-permute-start.3 = (bf16[16,8320]{1,0:T(8,128)(2,1)}, bf16[16,8320]{1,0:T(8,128)(2,1)S(1)}, u32[]{:S(2)}, u32[]{:S(2)}) collective-permute-start(bf16[16,8320]{1,0:T(8,128)(2,1)} %pack.1.refs_2_), channel_id=1, source_target_pairs={{0,14},{2,0},{4,2},{6,4},{8,6},{10,8},{12,10},{14,12},{16,18},{18,... | collective-permute-start | bytes 798728 | tf_op jit(solution)/shard_map/ppermute | solution.py:159
  34.2 11.8 %collective-permute-start.1 = (bf16[16,8320]{1,0:T(8,128)(2,1)S(1)}, bf16[16,8320]{1,0:T(8,128)(2,1)S(1)}, u32[]{:S(2)}, u32[]{:S(2)}) collective-permute-start(bf16[16,8320]{1,0:T(8,128)(2,1)S(1)} %collective-permute-done.refs_3_), channel_id=1, source_target_pairs={{0,2},{2,4},{4,6},{6,8},{8,10},{10,12},{12,14},{14,0},{16,30},{18,... | collective-permute-start | bytes 798728 | tf_op jit(solution)/shard_map/ppermute | solution.py:159
  37.2 38.0 %copy-start.2 = (bf16[16,8320]{1,0:T(8,128)(2,1)S(1)}, bf16[16,8320]{1,0:T(8,128)(2,1)}, u32[]{:S(2)}) copy-start(bf16[16,8320]{1,0:T(8,128)(2,1)} %pack.1.refs_2_) | copy-start | bytes 798724
  37.2 38.0 %copy-start.3 = (s32[1,2,64]{2,1,0:T(2,128)S(1)}, s32[1,2,64]{2,1,0:T(2,128)}, u32[]{:S(2)}) copy-start(s32[1,2,64]{2,1,0:T(2,128)} %param.9) | copy-start | bytes 1540
  46.3 25.3 %collective-permute-start.9 = (bf16[8192,128]{1,0:T(8,128)(2,1)S(1)}, bf16[8192,128]{1,0:T(8,128)(2,1)S(1)}, u32[]{:S(2)}, u32[]{:S(2)}) collective-permute-start(bf16[8192,128]{1,0:T(8,128)(2,1)S(1)} %constant_dynamic-update-slice_fusion), channel_id=1, source_target_pairs={{0,16},{16,0},{1,17},{17,1},{2,18},{18,2},{3,19},{19,3},{4,20},{20... | collective-permute-start | bytes 6291464 | tf_op jit(solution)/shard_map/ppermute | solution.py:190
  48.3 16.4 %collective-permute-start.8 = (bf16[16,8320]{1,0:T(8,128)(2,1)S(1)}, bf16[16,8320]{1,0:T(8,128)(2,1)}, u32[]{:S(2)}, u32[]{:S(2)}) collective-permute-start(bf16[16,8320]{1,0:T(8,128)(2,1)S(1)} %collective-permute-done.3.refs_4_), channel_id=1, source_target_pairs={{0,14},{2,0},{4,2},{6,4},{8,6},{10,8},{12,10},{14,12},{16,18},{18,... | collective-permute-start | bytes 798728 | tf_op jit(solution)/shard_map/ppermute | solution.py:159
  54.8 16.8 %collective-permute-start.7 = (bf16[16,8320]{1,0:T(8,128)(2,1)S(1)}, bf16[16,8320]{1,0:T(8,128)(2,1)S(1)}, u32[]{:S(2)}, u32[]{:S(2)}) collective-permute-start(bf16[16,8320]{1,0:T(8,128)(2,1)S(1)} %collective-permute-done.1.refs_5_), channel_id=1, source_target_pairs={{0,2},{2,4},{4,6},{6,8},{8,10},{10,12},{12,14},{14,0},{16,30},{18,... | collective-permute-start | bytes 798728 | tf_op jit(solution)/shard_map/ppermute | solution.py:159
  64.7 17.6 %collective-permute-start.10 = (bf16[16,8320]{1,0:T(8,128)(2,1)}, bf16[16,8320]{1,0:T(8,128)(2,1)}, u32[]{:S(2)}, u32[]{:S(2)}) collective-permute-start(bf16[16,8320]{1,0:T(8,128)(2,1)} %collective-permute-done.8.refs_6_), channel_id=1, source_target_pairs={{0,14},{2,0},{4,2},{6,4},{8,6},{10,8},{12,10},{14,12},{16,18},{18,... | collective-permute-start | bytes 798728 | tf_op jit(solution)/shard_map/ppermute | solution.py:159
  71.6 1.3 %copy-start = (bf16[8192,128]{1,0:T(8,128)(2,1)}, bf16[8192,128]{1,0:T(8,128)(2,1)S(1)}, u32[]{:S(2)}) copy-start(bf16[8192,128]{1,0:T(8,128)(2,1)S(1)} %collective-permute-done.9) | copy-start | bytes 6291460
  72.9 12.5 %collective-permute-start.11 = (bf16[16,8320]{1,0:T(8,128)(2,1)S(1)}, bf16[16,8320]{1,0:T(8,128)(2,1)}, u32[]{:S(2)}, u32[]{:S(2)}) collective-permute-start(bf16[16,8320]{1,0:T(8,128)(2,1)S(1)} %collective-permute-done.7.refs_2_), channel_id=1, source_target_pairs={{0,2},{2,4},{4,6},{6,8},{8,10},{10,12},{12,14},{14,0},{16,30},{18,... | collective-permute-start | bytes 798728 | tf_op jit(solution)/shard_map/ppermute | solution.py:159
  75.2 1.6 %copy-start.1 = (bf16[8192,128]{1,0:T(8,128)(2,1)S(1)}, bf16[8192,128]{1,0:T(8,128)(2,1)}, u32[]{:S(2)}) copy-start(bf16[8192,128]{1,0:T(8,128)(2,1)} %copy-done) | copy-start | bytes 6291460

commit v5 on v4

--- a/solution.py
+++ b/solution.py
@@ -180,8 +180,7 @@
     moved = [lax.ppermute(mine, "x", [(i, (i - k) % nx) for i in range(nx)]) for k in range(1, nx)]
     back.append(turn(back[0], -1))
     fwd.append(turn(fwd[1], 1))
-    back[1], fwd[1] = after(back[1], fwd[1])
-    back.append(turn(back[1], -1))
+    back.append(turn(back[0], -2))
     fwd[2], back[1], *moved = after(fwd[2], back[1], *moved)
     fwd.append(turn(fwd[2], 1))
     back[2], fwd[2] = after(back[2], fwd[2])

time: 106 us -> 115 us (1.085)
  the two profiles are of different devices: /device:TPU:2 before, /device:TPU:1 now
where the time goes in v5:
time: 115 us; the launch traced here: 114 us
  starting transfers between devices  60.6 us (53%)
  waiting for transfers between devices  25 us (22%)
  blocking collectives  12.3 us (11%)
  Pallas kernels  10.7 us (9%)
  local copies, waits for them, and re-layouts  4.32 us (4%)
    ppermute x7, starting transfers between devices, turn(): return lax.ppermute(v, ('core', 'zb'), pairs)  44.4 us
    ppermute x7, waiting for transfers between devices, turn(): return lax.ppermute(v, ('core', 'zb'), pairs)  18.5 us
    all_to_all x1, blocking collectives, body(): out = lax.all_to_all(out, ('layer', 'zc'), 0, 0, tiled=True)  12.3 us
    ppermute x3, starting transfers between devices, body(): lax.ppermute(mine, 'x', [(i, (i - k) % nx) for i in range(nx)])  9.46 us
    pallas_call x2, Pallas kernels, product(): pl.pallas_call(functools.partial(product_kernel, parts=parts, brows=brows...  7.3 us
    ppermute x3, waiting for transfers between devices, body(): lax.ppermute(mine, 'x', [(i, (i - k) % nx) for i in range(nx)])  6.46 us
    ppermute x1, starting transfers between devices, body(): far = lax.ppermute(mine, 'zc', [(0, 1), (1, 0)])  4.37 us
    unnamed x12, local copies, waits for them, and re-layouts  4.08 us
  transfers between devices with their start and end apart: 12, of which 6 were waited for; matrix products, arithmetic and copies ran while one was open for 2% of the time, Pallas kernels for 5%

profile of v5, /device:TPU:1, one launch (start us, length us, event | category | flops | bytes accessed | tf_op | source)
XLA Modules:
  0.0 114.2 jit_solution(15905738177904331137)
XLA Ops:
  0.0 4.4 %collective-permute-start.2 = (bf16[1024,128]{1,0:T(8,128)(2,1)}, bf16[1024,128]{1,0:T(8,128)(2,1)S(1)}, u32[]{:S(2)}, u32[]{:S(2)}) collective-permute-start(bf16[1024,128]{1,0:T(8,128)(2,1)} %bitcast.24), channel_id=1, source_target_pairs={{0,1},{1,0},{2,3},{3,2},{4,5},{5,4},{6,7},{7,6},{8,9},{9,8},{10,11... | collective-permute-start | bytes 786440 | tf_op jit(solution)/shard_map/ppermute | solution.py:176
  4.4 1.7 %pack.1.refs_2_ = bf16[16,8320]{1,0:T(8,128)(2,1)} custom-call(bf16[2,16,4096]{2,1,0:T(8,128)(2,1)} %bitcast.27, s32[2,16]{1,0:T(2,128)} %bitcast.28, s32[2]{0:T(128)} %bitcast.29), custom_call_target="tpu_custom_call" | custom-call | tf_op jit(solution)/shard_map/pack/pallas_call | solution.py:161
  6.1 10.7 %collective-permute-start = (bf16[16,8320]{1,0:T(8,128)(2,1)}, bf16[16,8320]{1,0:T(8,128)(2,1)S(1)}, u32[]{:S(2)}, u32[]{:S(2)}) collective-permute-start(bf16[16,8320]{1,0:T(8,128)(2,1)} %pack.1.refs_2_), channel_id=1, source_target_pairs={{0,2},{2,4},{4,6},{6,8},{8,10},{10,12},{12,14},{14,0},{16,30},{18,... | collective-permute-start | bytes 798728 | tf_op jit(solution)/shard_map/ppermute | solution.py:159
  17.7 4.5 %collective-permute-start.4 = (bf16[2048,128]{1,0:T(8,128)(2,1)S(1)}, bf16[2048,128]{1,0:T(8,128)(2,1)S(1)}, u32[]{:S(2)}, u32[]{:S(2)}) collective-permute-start(bf16[2048,128]{1,0:T(8,128)(2,1)S(1)} %pad_maximum_fusion), channel_id=1, source_target_pairs={{0,96},{32,0},{64,32},{96,64},{1,97},{33,1},{65,33},{97,65},{2,98}... | collective-permute-start | bytes 1572872 | tf_op jit(solution)/shard_map/ppermute | solution.py:180
  22.3 2.4 %collective-permute-start.5 = (bf16[2048,128]{1,0:T(8,128)(2,1)S(1)}, bf16[2048,128]{1,0:T(8,128)(2,1)S(1)}, u32[]{:S(2)}, u32[]{:S(2)}) collective-permute-start(bf16[2048,128]{1,0:T(8,128)(2,1)S(1)} %pad_maximum_fusion), channel_id=1, source_target_pairs={{0,64},{32,96},{64,0},{96,32},{1,65},{33,97},{65,1},{97,33},{2,66}... | collective-permute-start | bytes 1572872 | tf_op jit(solution)/shard_map/ppermute | solution.py:180
  24.7 2.5 %collective-permute-start.6 = (bf16[2048,128]{1,0:T(8,128)(2,1)S(1)}, bf16[2048,128]{1,0:T(8,128)(2,1)S(1)}, u32[]{:S(2)}, u32[]{:S(2)}) collective-permute-start(bf16[2048,128]{1,0:T(8,128)(2,1)S(1)} %pad_maximum_fusion), channel_id=1, source_target_pairs={{0,32},{32,64},{64,96},{96,0},{1,33},{33,65},{65,97},{97,1},{2,34}... | collective-permute-start | bytes 1572872 | tf_op jit(solution)/shard_map/ppermute | solution.py:180
  27.2 1.9 %collective-permute-start.3 = (bf16[16,8320]{1,0:T(8,128)(2,1)}, bf16[16,8320]{1,0:T(8,128)(2,1)S(1)}, u32[]{:S(2)}, u32[]{:S(2)}) collective-permute-start(bf16[16,8320]{1,0:T(8,128)(2,1)} %pack.1.refs_2_), channel_id=1, source_target_pairs={{0,14},{2,0},{4,2},{6,4},{8,6},{10,8},{12,10},{14,12},{16,18},{18,... | collective-permute-start | bytes 798728 | tf_op jit(solution)/shard_map/ppermute | solution.py:159
  29.2 5.5 %collective-permute-start.1 = (bf16[16,8320]{1,0:T(8,128)(2,1)S(1)}, bf16[16,8320]{1,0:T(8,128)(2,1)S(1)}, u32[]{:S(2)}, u32[]{:S(2)}) collective-permute-start(bf16[16,8320]{1,0:T(8,128)(2,1)S(1)} %collective-permute-done.refs_3_), channel_id=1, source_target_pairs={{0,2},{2,4},{4,6},{6,8},{8,10},{10,12},{12,14},{14,0},{16,30},{18,... | collective-permute-start | bytes 798728 | tf_op jit(solution)/shard_map/ppermute | solution.py:159
  35.7 2.5 %collective-permute-done.3.refs_4_ = bf16[16,8320]{1,0:T(8,128)(2,1)S(1)} collective-permute-done((bf16[16,8320]{1,0:T(8,128)(2,1)}, bf16[16,8320]{1,0:T(8,128)(2,1)S(1)}, u32[]{:S(2)}, u32[]{:S(2)}) %collective-permute-start.3) | collective-permute-done | bytes 266272 | tf_op jit(solution)/shard_map/ppermute | solution.py:159
  38.2 5.6 %collective-permute-done.1.refs_5_ = bf16[16,8320]{1,0:T(8,128)(2,1)S(1)} collective-permute-done((bf16[16,8320]{1,0:T(8,128)(2,1)S(1)}, bf16[16,8320]{1,0:T(8,128)(2,1)S(1)}, u32[]{:S(2)}, u32[]{:S(2)}) %collective-permute-start.1) | collective-permute-done | bytes 266272 | tf_op jit(solution)/shard_map/ppermute | solution.py:159
  44.4 5.9 %collective-permute-done.6 = bf16[2048,128]{1,0:T(8,128)(2,1)S(1)} collective-permute-done((bf16[2048,128]{1,0:T(8,128)(2,1)S(1)}, bf16[2048,128]{1,0:T(8,128)(2,1)S(1)}, u32[]{:S(2)}, u32[]{:S(2)}) %collective-permute-start.6) | collective-permute-done | bytes 524320 | tf_op jit(solution)/shard_map/ppermute | solution.py:180
  50.5 2.3 %collective-permute-start.9 = (bf16[8192,128]{1,0:T(8,128)(2,1)S(1)}, bf16[8192,128]{1,0:T(8,128)(2,1)S(1)}, u32[]{:S(2)}, u32[]{:S(2)}) collective-permute-start(bf16[8192,128]{1,0:T(8,128)(2,1)S(1)} %constant_dynamic-update-slice_fusion), channel_id=1, source_target_pairs={{0,16},{16,0},{1,17},{17,1},{2,18},{18,2},{3,19},{19,3},{4,20},{20... | collective-permute-start | bytes 6291464 | tf_op jit(solution)/shard_map/ppermute | solution.py:189
  52.8 3.1 %collective-permute-start.8 = (bf16[16,8320]{1,0:T(8,128)(2,1)S(1)}, bf16[16,8320]{1,0:T(8,128)(2,1)}, u32[]{:S(2)}, u32[]{:S(2)}) collective-permute-start(bf16[16,8320]{1,0:T(8,128)(2,1)S(1)} %copy-done.2), channel_id=1, source_target_pairs={{0,12},{2,14},{4,0},{6,2},{8,4},{10,6},{12,8},{14,10},{16,20},{18,... | collective-permute-start | bytes 798728 | tf_op jit(solution)/shard_map/ppermute | solution.py:159
  56.0 4.3 %collective-permute-start.7 = (bf16[16,8320]{1,0:T(8,128)(2,1)S(1)}, bf16[16,8320]{1,0:T(8,128)(2,1)S(1)}, u32[]{:S(2)}, u32[]{:S(2)}) collective-permute-start(bf16[16,8320]{1,0:T(8,128)(2,1)S(1)} %collective-permute-done.1.refs_5_), channel_id=1, source_target_pairs={{0,2},{2,4},{4,6},{6,8},{8,10},{10,12},{12,14},{14,0},{16,30},{18,... | collective-permute-start | bytes 798728 | tf_op jit(solution)/shard_map/ppermute | solution.py:159
  60.3 5.9 %collective-permute-done.8.refs_6_ = bf16[16,8320]{1,0:T(8,128)(2,1)} collective-permute-done((bf16[16,8320]{1,0:T(8,128)(2,1)S(1)}, bf16[16,8320]{1,0:T(8,128)(2,1)}, u32[]{:S(2)}, u32[]{:S(2)}) %collective-permute-start.8) | collective-permute-done | bytes 266272 | tf_op jit(solution)/shard_map/ppermute | solution.py:159
  66.1 13.3 %collective-permute-start.10 = (bf16[16,8320]{1,0:T(8,128)(2,1)}, bf16[16,8320]{1,0:T(8,128)(2,1)}, u32[]{:S(2)}, u32[]{:S(2)}) collective-permute-start(bf16[16,8320]{1,0:T(8,128)(2,1)} %collective-permute-done.8.refs_6_), channel_id=1, source_target_pairs={{0,14},{2,0},{4,2},{6,4},{8,6},{10,8},{12,10},{14,12},{16,18},{18,... | collective-permute-start | bytes 798728 | tf_op jit(solution)/shard_map/ppermute | solution.py:159
  79.5 1.3 %copy-done = bf16[8192,128]{1,0:T(8,128)(2,1)} copy-done((bf16[8192,128]{1,0:T(8,128)(2,1)}, bf16[8192,128]{1,0:T(8,128)(2,1)S(1)}, u32[]{:S(2)}) %copy-start) | copy-done | bytes 2097176
  80.8 5.7 %collective-permute-start.11 = (bf16[16,8320]{1,0:T(8,128)(2,1)S(1)}, bf16[16,8320]{1,0:T(8,128)(2,1)}, u32[]{:S(2)}, u32[]{:S(2)}) collective-permute-start(bf16[16,8320]{1,0:T(8,128)(2,1)S(1)} %collective-permute-done.7.refs_2_), channel_id=1, source_target_pairs={{0,2},{2,4},{4,6},{6,8},{8,10},{10,12},{12,14},{14,0},{16,30},{18,... | collective-permute-start | bytes 798728 | tf_op jit(solution)/shard_map/ppermute | solution.py:159
  86.8 1.6 %copy-done.1 = bf16[8192,128]{1,0:T(8,128)(2,1)S(1)} copy-done((bf16[8192,128]{1,0:T(8,128)(2,1)S(1)}, bf16[8192,128]{1,0:T(8,128)(2,1)}, u32[]{:S(2)}) %copy-start.1) | copy-done | bytes 2097176
  88.4 4.2 %product.1.refs_7_ = f32[4,256,128]{2,1,0:T(8,128)S(1)} custom-call(s32[2,64]{1,0:T(2,128)S(1)} %bitcast.22, s32[8]{0:T(128)S(1)} %stack.54.refs_1_, bf16[16,8320]{1,0:T(8,128)(2,1)S(1)} %copy-done.2, bf16[16,8320]{1,0:T(8,128)(2,1)S(1)} %collective-permute-done.refs_3_, bf16[16,8320]{1,0:T(8,128)(2,1)S(1)} %collective-permute-done.3.refs_4_, ...), custom_call_target="tpu_custom_call" | custom-call | flops 1342177280 | bytes 8388608 | tf_op jit(solution)/shard_map/product/pallas_call | solution.py:111
  92.6 4.5 %collective-permute-done.11.refs_4_ = bf16[16,8320]{1,0:T(8,128)(2,1)} collective-permute-done((bf16[16,8320]{1,0:T(8,128)(2,1)S(1)}, bf16[16,8320]{1,0:T(8,128)(2,1)}, u32[]{:S(2)}, u32[]{:S(2)}) %collective-permute-start.11) | collective-permute-done | bytes 266272 | tf_op jit(solution)/shard_map/ppermute | solution.py:159
  97.1 3.1 %product_last.1 = f32[8,64,256]{2,1,0:T(8,128)S(1)} custom-call(s32[2,64]{1,0:T(2,128)S(1)} %bitcast.23, s32[6]{0:T(128)S(1)} %stack.48.refs_1_, bf16[16,8320]{1,0:T(8,128)(2,1)S(1)} %collective-permute-done.7.refs_2_, bf16[16,8320]{1,0:T(8,128)(2,1)} %collective-permute-done.10.refs_3_, bf16[16,8320]{1,0:T(8,128)(2,1)} %collective-permute-done.11.refs_4_, ...), custom_call_target="tpu_custom_call" | custom-call | flops 805306368 | bytes 8388608 | tf_op jit(solution)/shard_map/product_last/pallas_call | solution.py:111
  100.2 12.3 %all_to_all.5.parts_ref = f32[8,64,256]{2,1,0:T(8,128)} all-to-all(f32[8,64,256]{2,1,0:T(8,128)S(1)} %product_last.1), channel_id=1, replica_groups=mesh['layer'=4,'x'=4,'core'=2,'zb'=8,'zc'=2] {'layer','zc'}, dimensions={0} | all-to-all | bytes 1048576 | tf_op jit(solution)/shard_map/all_to_all | solution.py:212
  112.5 1.7 %finish.1 = bf16[128,128]{1,0:T(8,128)(2,1)} custom-call(f32[8,64,256]{2,1,0:T(8,128)} %all_to_all.5.parts_ref), custom_call_target="tpu_custom_call" | custom-call | tf_op jit(solution)/shard_map/finish/pallas_call | solution.py:213
  (21 shorter events, 3.0 us)
Async XLA Ops:
  0.0 16.7 %collective-permute-start.2 = (bf16[1024,128]{1,0:T(8,128)(2,1)}, bf16[1024,128]{1,0:T(8,128)(2,1)S(1)}, u32[]{:S(2)}, u32[]{:S(2)}) collective-permute-start(bf16[1024,128]{1,0:T(8,128)(2,1)} %bitcast.24), channel_id=1, source_target_pairs={{0,1},{1,0},{2,3},{3,2},{4,5},{5,4},{6,7},{7,6},{8,9},{9,8},{10,11... | collective-permute-start | bytes 786440 | tf_op jit(solution)/shard_map/ppermute | solution.py:176
  6.1 23.1 %collective-permute-start = (bf16[16,8320]{1,0:T(8,128)(2,1)}, bf16[16,8320]{1,0:T(8,128)(2,1)S(1)}, u32[]{:S(2)}, u32[]{:S(2)}) collective-permute-start(bf16[16,8320]{1,0:T(8,128)(2,1)} %pack.1.refs_2_), channel_id=1, source_target_pairs={{0,2},{2,4},{4,6},{6,8},{8,10},{10,12},{12,14},{14,0},{16,30},{18,... | collective-permute-start | bytes 798728 | tf_op jit(solution)/shard_map/ppermute | solution.py:159
  17.7 35.1 %copy-start.2 = (bf16[16,8320]{1,0:T(8,128)(2,1)S(1)}, bf16[16,8320]{1,0:T(8,128)(2,1)}, u32[]{:S(2)}) copy-start(bf16[16,8320]{1,0:T(8,128)(2,1)} %pack.1.refs_2_) | copy-start | bytes 798724
  17.7 26.6 %collective-permute-start.4 = (bf16[2048,128]{1,0:T(8,128)(2,1)S(1)}, bf16[2048,128]{1,0:T(8,128)(2,1)S(1)}, u32[]{:S(2)}, u32[]{:S(2)}) collective-permute-start(bf16[2048,128]{1,0:T(8,128)(2,1)S(1)} %pad_maximum_fusion), channel_id=1, source_target_pairs={{0,96},{32,0},{64,32},{96,64},{1,97},{33,1},{65,33},{97,65},{2,98}... | collective-permute-start | bytes 1572872 | tf_op jit(solution)/shard_map/ppermute | solution.py:180
  22.3 22.1 %collective-permute-start.5 = (bf16[2048,128]{1,0:T(8,128)(2,1)S(1)}, bf16[2048,128]{1,0:T(8,128)(2,1)S(1)}, u32[]{:S(2)}, u32[]{:S(2)}) collective-permute-start(bf16[2048,128]{1,0:T(8,128)(2,1)S(1)} %pad_maximum_fusion), channel_id=1, source_target_pairs={{0,64},{32,96},{64,0},{96,32},{1,65},{33,97},{65,1},{97,33},{2,66}... | collective-permute-start | bytes 1572872 | tf_op jit(solution)/shard_map/ppermute | solution.py:180
  24.7 25.5 %collective-permute-start.6 = (bf16[2048,128]{1,0:T(8,128)(2,1)S(1)}, bf16[2048,128]{1,0:T(8,128)(2,1)S(1)}, u32[]{:S(2)}, u32[]{:S(2)}) collective-permute-start(bf16[2048,128]{1,0:T(8,128)(2,1)S(1)} %pad_maximum_fusion), channel_id=1, source_target_pairs={{0,32},{32,64},{64,96},{96,0},{1,33},{33,65},{65,97},{97,1},{2,34}... | collective-permute-start | bytes 1572872 | tf_op jit(solution)/shard_map/ppermute | solution.py:180
  27.2 10.9 %collective-permute-start.3 = (bf16[16,8320]{1,0:T(8,128)(2,1)}, bf16[16,8320]{1,0:T(8,128)(2,1)S(1)}, u32[]{:S(2)}, u32[]{:S(2)}) collective-permute-start(bf16[16,8320]{1,0:T(8,128)(2,1)} %pack.1.refs_2_), channel_id=1, source_target_pairs={{0,14},{2,0},{4,2},{6,4},{8,6},{10,8},{12,10},{14,12},{16,18},{18,... | collective-permute-start | bytes 798728 | tf_op jit(solution)/shard_map/ppermute | solution.py:159
  29.2 14.6 %collective-permute-start.1 = (bf16[16,8320]{1,0:T(8,128)(2,1)S(1)}, bf16[16,8320]{1,0:T(8,128)(2,1)S(1)}, u32[]{:S(2)}, u32[]{:S(2)}) collective-permute-start(bf16[16,8320]{1,0:T(8,128)(2,1)S(1)} %collective-permute-done.refs_3_), channel_id=1, source_target_pairs={{0,2},{2,4},{4,6},{6,8},{8,10},{10,12},{12,14},{14,0},{16,30},{18,... | collective-permute-start | bytes 798728 | tf_op jit(solution)/shard_map/ppermute | solution.py:159
  35.6 51.2 %copy-start.3 = (s32[1,2,64]{2,1,0:T(2,128)S(1)}, s32[1,2,64]{2,1,0:T(2,128)}, u32[]{:S(2)}) copy-start(s32[1,2,64]{2,1,0:T(2,128)} %param.9) | copy-start | bytes 1540
  50.5 29.0 %collective-permute-start.9 = (bf16[8192,128]{1,0:T(8,128)(2,1)S(1)}, bf16[8192,128]{1,0:T(8,128)(2,1)S(1)}, u32[]{:S(2)}, u32[]{:S(2)}) collective-permute-start(bf16[8192,128]{1,0:T(8,128)(2,1)S(1)} %constant_dynamic-update-slice_fusion), channel_id=1, source_target_pairs={{0,16},{16,0},{1,17},{17,1},{2,18},{18,2},{3,19},{19,3},{4,20},{20... | collective-permute-start | bytes 6291464 | tf_op jit(solution)/shard_map/ppermute | solution.py:189
  52.8 13.3 %collective-permute-start.8 = (bf16[16,8320]{1,0:T(8,128)(2,1)S(1)}, bf16[16,8320]{1,0:T(8,128)(2,1)}, u32[]{:S(2)}, u32[]{:S(2)}) collective-permute-start(bf16[16,8320]{1,0:T(8,128)(2,1)S(1)} %copy-done.2), channel_id=1, source_target_pairs={{0,12},{2,14},{4,0},{6,2},{8,4},{10,6},{12,8},{14,10},{16,20},{18,... | collective-permute-start | bytes 798728 | tf_op jit(solution)/shard_map/ppermute | solution.py:159
  56.0 23.5 %collective-permute-start.7 = (bf16[16,8320]{1,0:T(8,128)(2,1)S(1)}, bf16[16,8320]{1,0:T(8,128)(2,1)S(1)}, u32[]{:S(2)}, u32[]{:S(2)}) collective-permute-start(bf16[16,8320]{1,0:T(8,128)(2,1)S(1)} %collective-permute-done.1.refs_5_), channel_id=1, source_target_pairs={{0,2},{2,4},{4,6},{6,8},{8,10},{10,12},{12,14},{14,0},{16,30},{18,... | collective-permute-start | bytes 798728 | tf_op jit(solution)/shard_map/ppermute | solution.py:159
  66.1 26.5 %collective-permute-start.10 = (bf16[16,8320]{1,0:T(8,128)(2,1)}, bf16[16,8320]{1,0:T(8,128)(2,1)}, u32[]{:S(2)}, u32[]{:S(2)}) collective-permute-start(bf16[16,8320]{1,0:T(8,128)(2,1)} %collective-permute-done.8.refs_6_), channel_id=1, source_target_pairs={{0,14},{2,0},{4,2},{6,4},{8,6},{10,8},{12,10},{14,12},{16,18},{18,... | collective-permute-start | bytes 798728 | tf_op jit(solution)/shard_map/ppermute | solution.py:159
  79.5 1.3 %copy-start = (bf16[8192,128]{1,0:T(8,128)(2,1)}, bf16[8192,128]{1,0:T(8,128)(2,1)S(1)}, u32[]{:S(2)}) copy-start(bf16[8192,128]{1,0:T(8,128)(2,1)S(1)} %collective-permute-done.9) | copy-start | bytes 6291460
  80.8 16.3 %collective-permute-start.11 = (bf16[16,8320]{1,0:T(8,128)(2,1)S(1)}, bf16[16,8320]{1,0:T(8,128)(2,1)}, u32[]{:S(2)}, u32[]{:S(2)}) collective-permute-start(bf16[16,8320]{1,0:T(8,128)(2,1)S(1)} %collective-permute-done.7.refs_2_), channel_id=1, source_target_pairs={{0,2},{2,4},{4,6},{6,8},{8,10},{10,12},{12,14},{14,0},{16,30},{18,... | collective-permute-start | bytes 798728 | tf_op jit(solution)/shard_map/ppermute | solution.py:159
  86.8 1.6 %copy-start.1 = (bf16[8192,128]{1,0:T(8,128)(2,1)S(1)}, bf16[8192,128]{1,0:T(8,128)(2,1)}, u32[]{:S(2)}) copy-start(bf16[8192,128]{1,0:T(8,128)(2,1)} %copy-done) | copy-start | bytes 6291460

commit v6 on v2

--- a/solution.py
+++ b/solution.py
@@ -122,11 +122,11 @@
         functools.partial(
             product_kernel, parts=parts, brows=brows, slots=slots, blks=blks, group=group, first=first, last=last
         ),
-        in_specs=[smem, smem] + [vmem] * len(pieces) + [pl.BlockSpec(memory_space=pl.ANY)] * 2 + [vmem] * (not first),
+        in_specs=[smem, smem] + [vmem] * len(pieces) + [pl.BlockSpec(memory_space=pltpu.HBM)] * 2 + [vmem] * (not first),
         out_specs=vmem,
         scratch_shapes=scratch,
         out_shape=outs if last else sums,
-        compiler_params=pltpu.CompilerParams(vmem_limit_bytes=48 * 1024 * 1024),
+        compiler_params=pltpu.CompilerParams(vmem_limit_bytes=20 * 1024 * 1024),
         cost_estimate=pl.CostEstimate(flops=2 * macs, bytes_accessed=8 << 20, transcendentals=0),
         name="product_last" if last else "product",
     )(own, nums, *pieces, *b, *([] if first else [acc]))

time: 106 us -> 106 us (level)
  no operation moved by 1% of the time
where the time goes in v6:
time: 106 us
  starting transfers between devices  52.5 us (50%)
  waiting for transfers between devices  21 us (20%)
  blocking collectives  15.1 us (14%)
  Pallas kernels  11.3 us (11%)
  local copies, waits for them, and re-layouts  4.31 us (4%)
    ppermute x7, starting transfers between devices, turn(): return lax.ppermute(v, ('core', 'zb'), pairs)  33 us
    ppermute x7, waiting for transfers between devices, turn(): return lax.ppermute(v, ('core', 'zb'), pairs)  21 us
    all_to_all x1, blocking collectives, body(): out = lax.all_to_all(out, ('layer', 'zc'), 0, 0, tiled=True)  15.1 us
    ppermute x3, starting transfers between devices, body(): lax.ppermute(mine, 'x', [(i, (i - k) % nx) for i in range(nx)])  13.7 us
    pallas_call x2, Pallas kernels, product(): pl.pallas_call(functools.partial(product_kernel, parts=parts, brows=brows...  7.91 us
    unnamed x12, local copies, waits for them, and re-layouts  4.07 us
    ppermute x1, starting transfers between devices, body(): far = lax.ppermute(mine, 'zc', [(0, 1), (1, 0)])  3.82 us
  transfers between devices with their start and end apart: 12, of which 5 were waited for; matrix products, arithmetic and copies ran while one was open for 2% of the time, Pallas kernels for 6%

profile of v6, /device:TPU:2, one launch (start us, length us, event | category | flops | bytes accessed | tf_op | source)
XLA Modules:
  0.0 105.6 jit_solution(6806946062515338692)
XLA Ops:
  0.0 3.8 %collective-permute-start.2 = (bf16[1024,128]{1,0:T(8,128)(2,1)}, bf16[1024,128]{1,0:T(8,128)(2,1)S(1)}, u32[]{:S(2)}, u32[]{:S(2)}) collective-permute-start(bf16[1024,128]{1,0:T(8,128)(2,1)} %bitcast.24), channel_id=1, source_target_pairs={{0,1},{1,0},{2,3},{3,2},{4,5},{5,4},{6,7},{7,6},{8,9},{9,8},{10,11... | collective-permute-start | bytes 786440 | tf_op jit(solution)/shard_map/ppermute | solution.py:186
  3.8 1.7 %pack.1.refs_2_ = bf16[16,8320]{1,0:T(8,128)(2,1)} custom-call(bf16[2,16,4096]{2,1,0:T(8,128)(2,1)} %bitcast.27, s32[2,16]{1,0:T(2,128)} %bitcast.28, s32[2]{0:T(128)} %bitcast.29), custom_call_target="tpu_custom_call" | custom-call | tf_op jit(solution)/shard_map/pack/pallas_call | solution.py:171
  5.5 5.2 %collective-permute-start = (bf16[16,8320]{1,0:T(8,128)(2,1)}, bf16[16,8320]{1,0:T(8,128)(2,1)S(1)}, u32[]{:S(2)}, u32[]{:S(2)}) collective-permute-start(bf16[16,8320]{1,0:T(8,128)(2,1)} %pack.1.refs_2_), channel_id=1, source_target_pairs={{0,2},{2,4},{4,6},{6,8},{8,10},{10,12},{12,14},{14,0},{16,30},{18,... | collective-permute-start | bytes 798728 | tf_op jit(solution)/shard_map/ppermute | solution.py:169
  10.7 1.0 pad_maximum_fusion
  11.7 8.4 %collective-permute-start.4 = (bf16[2048,128]{1,0:T(8,128)(2,1)S(1)}, bf16[2048,128]{1,0:T(8,128)(2,1)S(1)}, u32[]{:S(2)}, u32[]{:S(2)}) collective-permute-start(bf16[2048,128]{1,0:T(8,128)(2,1)S(1)} %pad_maximum_fusion), channel_id=1, source_target_pairs={{0,96},{32,0},{64,32},{96,64},{1,97},{33,1},{65,33},{97,65},{2,98}... | collective-permute-start | bytes 1572872 | tf_op jit(solution)/shard_map/ppermute | solution.py:190
  20.1 1.9 %collective-permute-start.5 = (bf16[2048,128]{1,0:T(8,128)(2,1)S(1)}, bf16[2048,128]{1,0:T(8,128)(2,1)S(1)}, u32[]{:S(2)}, u32[]{:S(2)}) collective-permute-start(bf16[2048,128]{1,0:T(8,128)(2,1)S(1)} %pad_maximum_fusion), channel_id=1, source_target_pairs={{0,64},{32,96},{64,0},{96,32},{1,65},{33,97},{65,1},{97,33},{2,66}... | collective-permute-start | bytes 1572872 | tf_op jit(solution)/shard_map/ppermute | solution.py:190
  22.1 3.4 %collective-permute-start.6 = (bf16[2048,128]{1,0:T(8,128)(2,1)S(1)}, bf16[2048,128]{1,0:T(8,128)(2,1)S(1)}, u32[]{:S(2)}, u32[]{:S(2)}) collective-permute-start(bf16[2048,128]{1,0:T(8,128)(2,1)S(1)} %pad_maximum_fusion), channel_id=1, source_target_pairs={{0,32},{32,64},{64,96},{96,0},{1,33},{33,65},{65,97},{97,1},{2,34}... | collective-permute-start | bytes 1572872 | tf_op jit(solution)/shard_map/ppermute | solution.py:190
  25.4 8.8 %collective-permute-start.3 = (bf16[16,8320]{1,0:T(8,128)(2,1)}, bf16[16,8320]{1,0:T(8,128)(2,1)S(1)}, u32[]{:S(2)}, u32[]{:S(2)}) collective-permute-start(bf16[16,8320]{1,0:T(8,128)(2,1)} %pack.1.refs_2_), channel_id=1, source_target_pairs={{0,14},{2,0},{4,2},{6,4},{8,6},{10,8},{12,10},{14,12},{16,18},{18,... | collective-permute-start | bytes 798728 | tf_op jit(solution)/shard_map/ppermute | solution.py:169
  34.2 1.9 %collective-permute-start.1 = (bf16[16,8320]{1,0:T(8,128)(2,1)S(1)}, bf16[16,8320]{1,0:T(8,128)(2,1)S(1)}, u32[]{:S(2)}, u32[]{:S(2)}) collective-permute-start(bf16[16,8320]{1,0:T(8,128)(2,1)S(1)} %collective-permute-done.refs_3_), channel_id=1, source_target_pairs={{0,2},{2,4},{4,6},{6,8},{8,10},{10,12},{12,14},{14,0},{16,30},{18,... | collective-permute-start | bytes 798728 | tf_op jit(solution)/shard_map/ppermute | solution.py:169
  37.2 8.6 %collective-permute-done.3.refs_4_ = bf16[16,8320]{1,0:T(8,128)(2,1)S(1)} collective-permute-done((bf16[16,8320]{1,0:T(8,128)(2,1)}, bf16[16,8320]{1,0:T(8,128)(2,1)S(1)}, u32[]{:S(2)}, u32[]{:S(2)}) %collective-permute-start.3) | collective-permute-done | bytes 266272 | tf_op jit(solution)/shard_map/ppermute | solution.py:169
  46.3 2.0 %collective-permute-start.9 = (bf16[8192,128]{1,0:T(8,128)(2,1)S(1)}, bf16[8192,128]{1,0:T(8,128)(2,1)S(1)}, u32[]{:S(2)}, u32[]{:S(2)}) collective-permute-start(bf16[8192,128]{1,0:T(8,128)(2,1)S(1)} %constant_dynamic-update-slice_fusion), channel_id=1, source_target_pairs={{0,16},{16,0},{1,17},{17,1},{2,18},{18,2},{3,19},{19,3},{4,20},{20... | collective-permute-start | bytes 6291464 | tf_op jit(solution)/shard_map/ppermute | solution.py:200
  48.3 6.5 %collective-permute-start.8 = (bf16[16,8320]{1,0:T(8,128)(2,1)S(1)}, bf16[16,8320]{1,0:T(8,128)(2,1)}, u32[]{:S(2)}, u32[]{:S(2)}) collective-permute-start(bf16[16,8320]{1,0:T(8,128)(2,1)S(1)} %collective-permute-done.3.refs_4_), channel_id=1, source_target_pairs={{0,14},{2,0},{4,2},{6,4},{8,6},{10,8},{12,10},{14,12},{16,18},{18,... | collective-permute-start | bytes 798728 | tf_op jit(solution)/shard_map/ppermute | solution.py:169
  54.8 1.9 %collective-permute-start.7 = (bf16[16,8320]{1,0:T(8,128)(2,1)S(1)}, bf16[16,8320]{1,0:T(8,128)(2,1)S(1)}, u32[]{:S(2)}, u32[]{:S(2)}) collective-permute-start(bf16[16,8320]{1,0:T(8,128)(2,1)S(1)} %collective-permute-done.1.refs_5_), channel_id=1, source_target_pairs={{0,2},{2,4},{4,6},{6,8},{8,10},{10,12},{12,14},{14,0},{16,30},{18,... | collective-permute-start | bytes 798728 | tf_op jit(solution)/shard_map/ppermute | solution.py:169
  56.7 8.0 %collective-permute-done.8.refs_6_ = bf16[16,8320]{1,0:T(8,128)(2,1)} collective-permute-done((bf16[16,8320]{1,0:T(8,128)(2,1)S(1)}, bf16[16,8320]{1,0:T(8,128)(2,1)}, u32[]{:S(2)}, u32[]{:S(2)}) %collective-permute-start.8) | collective-permute-done | bytes 266272 | tf_op jit(solution)/shard_map/ppermute | solution.py:169
  64.7 6.8 %collective-permute-start.10 = (bf16[16,8320]{1,0:T(8,128)(2,1)}, bf16[16,8320]{1,0:T(8,128)(2,1)}, u32[]{:S(2)}, u32[]{:S(2)}) collective-permute-start(bf16[16,8320]{1,0:T(8,128)(2,1)} %collective-permute-done.8.refs_6_), channel_id=1, source_target_pairs={{0,14},{2,0},{4,2},{6,4},{8,6},{10,8},{12,10},{14,12},{16,18},{18,... | collective-permute-start | bytes 798728 | tf_op jit(solution)/shard_map/ppermute | solution.py:169
  71.6 1.3 %copy-done = bf16[8192,128]{1,0:T(8,128)(2,1)} copy-done((bf16[8192,128]{1,0:T(8,128)(2,1)}, bf16[8192,128]{1,0:T(8,128)(2,1)S(1)}, u32[]{:S(2)}) %copy-start) | copy-done | bytes 2097176
  72.9 1.9 %collective-permute-start.11 = (bf16[16,8320]{1,0:T(8,128)(2,1)S(1)}, bf16[16,8320]{1,0:T(8,128)(2,1)}, u32[]{:S(2)}, u32[]{:S(2)}) collective-permute-start(bf16[16,8320]{1,0:T(8,128)(2,1)S(1)} %collective-permute-done.7.refs_2_), channel_id=1, source_target_pairs={{0,2},{2,4},{4,6},{6,8},{8,10},{10,12},{12,14},{14,0},{16,30},{18,... | collective-permute-start | bytes 798728 | tf_op jit(solution)/shard_map/ppermute | solution.py:169
  75.2 1.6 %copy-done.1 = bf16[8192,128]{1,0:T(8,128)(2,1)S(1)} copy-done((bf16[8192,128]{1,0:T(8,128)(2,1)S(1)}, bf16[8192,128]{1,0:T(8,128)(2,1)}, u32[]{:S(2)}) %copy-start.1) | copy-done | bytes 2097176
  76.8 4.5 %product.1.refs_7_ = f32[4,256,128]{2,1,0:T(8,128)S(1)} custom-call(s32[2,64]{1,0:T(2,128)S(1)} %bitcast.22, s32[8]{0:T(128)S(1)} %stack.54.refs_1_, bf16[16,8320]{1,0:T(8,128)(2,1)S(1)} %copy-done.2, bf16[16,8320]{1,0:T(8,128)(2,1)S(1)} %collective-permute-done.refs_3_, bf16[16,8320]{1,0:T(8,128)(2,1)S(1)} %collective-permute-done.3.refs_4_, ...), custom_call_target="tpu_custom_call" | custom-call | flops 1342177280 | bytes 8388608 | tf_op jit(solution)/shard_map/product/pallas_call | solution.py:121
  81.3 1.1 collective-permute-done.10.refs_3_
  82.3 3.1 %collective-permute-done.11.refs_4_ = bf16[16,8320]{1,0:T(8,128)(2,1)} collective-permute-done((bf16[16,8320]{1,0:T(8,128)(2,1)S(1)}, bf16[16,8320]{1,0:T(8,128)(2,1)}, u32[]{:S(2)}, u32[]{:S(2)}) %collective-permute-start.11) | collective-permute-done | bytes 266272 | tf_op jit(solution)/shard_map/ppermute | solution.py:169
  85.5 3.4 %product_last.1 = f32[8,64,256]{2,1,0:T(8,128)S(1)} custom-call(s32[2,64]{1,0:T(2,128)S(1)} %bitcast.23, s32[6]{0:T(128)S(1)} %stack.48.refs_1_, bf16[16,8320]{1,0:T(8,128)(2,1)S(1)} %collective-permute-done.7.refs_2_, bf16[16,8320]{1,0:T(8,128)(2,1)} %collective-permute-done.10.refs_3_, bf16[16,8320]{1,0:T(8,128)(2,1)} %collective-permute-done.11.refs_4_, ...), custom_call_target="tpu_custom_call" | custom-call | flops 805306368 | bytes 8388608 | tf_op jit(solution)/shard_map/product_last/pallas_call | solution.py:121
  88.9 15.1 %all_to_all.5.parts_ref = f32[8,64,256]{2,1,0:T(8,128)} all-to-all(f32[8,64,256]{2,1,0:T(8,128)S(1)} %product_last.1), channel_id=1, replica_groups=mesh['layer'=4,'x'=4,'core'=2,'zb'=8,'zc'=2] {'layer','zc'}, dimensions={0} | all-to-all | bytes 1048576 | tf_op jit(solution)/shard_map/all_to_all | solution.py:223
  103.9 1.7 %finish.1 = bf16[128,128]{1,0:T(8,128)(2,1)} custom-call(f32[8,64,256]{2,1,0:T(8,128)} %all_to_all.5.parts_ref), custom_call_target="tpu_custom_call" | custom-call | tf_op jit(solution)/shard_map/finish/pallas_call | solution.py:224
  (21 shorter events, 1.7 us)
Async XLA Ops:
  0.0 10.7 %collective-permute-start.2 = (bf16[1024,128]{1,0:T(8,128)(2,1)}, bf16[1024,128]{1,0:T(8,128)(2,1)S(1)}, u32[]{:S(2)}, u32[]{:S(2)}) collective-permute-start(bf16[1024,128]{1,0:T(8,128)(2,1)} %bitcast.24), channel_id=1, source_target_pairs={{0,1},{1,0},{2,3},{3,2},{4,5},{5,4},{6,7},{7,6},{8,9},{9,8},{10,11... | collective-permute-start | bytes 786440 | tf_op jit(solution)/shard_map/ppermute | solution.py:186
  5.5 28.7 %collective-permute-start = (bf16[16,8320]{1,0:T(8,128)(2,1)}, bf16[16,8320]{1,0:T(8,128)(2,1)S(1)}, u32[]{:S(2)}, u32[]{:S(2)}) collective-permute-start(bf16[16,8320]{1,0:T(8,128)(2,1)} %pack.1.refs_2_), channel_id=1, source_target_pairs={{0,2},{2,4},{4,6},{6,8},{8,10},{10,12},{12,14},{14,0},{16,30},{18,... | collective-permute-start | bytes 798728 | tf_op jit(solution)/shard_map/ppermute | solution.py:169
  11.7 34.3 %collective-permute-start.4 = (bf16[2048,128]{1,0:T(8,128)(2,1)S(1)}, bf16[2048,128]{1,0:T(8,128)(2,1)S(1)}, u32[]{:S(2)}, u32[]{:S(2)}) collective-permute-start(bf16[2048,128]{1,0:T(8,128)(2,1)S(1)} %pad_maximum_fusion), channel_id=1, source_target_pairs={{0,96},{32,0},{64,32},{96,64},{1,97},{33,1},{65,33},{97,65},{2,98}... | collective-permute-start | bytes 1572872 | tf_op jit(solution)/shard_map/ppermute | solution.py:190
  20.1 25.9 %collective-permute-start.5 = (bf16[2048,128]{1,0:T(8,128)(2,1)S(1)}, bf16[2048,128]{1,0:T(8,128)(2,1)S(1)}, u32[]{:S(2)}, u32[]{:S(2)}) collective-permute-start(bf16[2048,128]{1,0:T(8,128)(2,1)S(1)} %pad_maximum_fusion), channel_id=1, source_target_pairs={{0,64},{32,96},{64,0},{96,32},{1,65},{33,97},{65,1},{97,33},{2,66}... | collective-permute-start | bytes 1572872 | tf_op jit(solution)/shard_map/ppermute | solution.py:190
  22.1 24.0 %collective-permute-start.6 = (bf16[2048,128]{1,0:T(8,128)(2,1)S(1)}, bf16[2048,128]{1,0:T(8,128)(2,1)S(1)}, u32[]{:S(2)}, u32[]{:S(2)}) collective-permute-start(bf16[2048,128]{1,0:T(8,128)(2,1)S(1)} %pad_maximum_fusion), channel_id=1, source_target_pairs={{0,32},{32,64},{64,96},{96,0},{1,33},{33,65},{65,97},{97,1},{2,34}... | collective-permute-start | bytes 1572872 | tf_op jit(solution)/shard_map/ppermute | solution.py:190
  25.4 20.3 %collective-permute-start.3 = (bf16[16,8320]{1,0:T(8,128)(2,1)}, bf16[16,8320]{1,0:T(8,128)(2,1)S(1)}, u32[]{:S(2)}, u32[]{:S(2)}) collective-permute-start(bf16[16,8320]{1,0:T(8,128)(2,1)} %pack.1.refs_2_), channel_id=1, source_target_pairs={{0,14},{2,0},{4,2},{6,4},{8,6},{10,8},{12,10},{14,12},{16,18},{18,... | collective-permute-start | bytes 798728 | tf_op jit(solution)/shard_map/ppermute | solution.py:169
  34.2 11.8 %collective-permute-start.1 = (bf16[16,8320]{1,0:T(8,128)(2,1)S(1)}, bf16[16,8320]{1,0:T(8,128)(2,1)S(1)}, u32[]{:S(2)}, u32[]{:S(2)}) collective-permute-start(bf16[16,8320]{1,0:T(8,128)(2,1)S(1)} %collective-permute-done.refs_3_), channel_id=1, source_target_pairs={{0,2},{2,4},{4,6},{6,8},{8,10},{10,12},{12,14},{14,0},{16,30},{18,... | collective-permute-start | bytes 798728 | tf_op jit(solution)/shard_map/ppermute | solution.py:169
  37.2 38.0 %copy-start.2 = (bf16[16,8320]{1,0:T(8,128)(2,1)S(1)}, bf16[16,8320]{1,0:T(8,128)(2,1)}, u32[]{:S(2)}) copy-start(bf16[16,8320]{1,0:T(8,128)(2,1)} %pack.1.refs_2_) | copy-start | bytes 798724
  37.2 38.0 %copy-start.3 = (s32[1,2,64]{2,1,0:T(2,128)S(1)}, s32[1,2,64]{2,1,0:T(2,128)}, u32[]{:S(2)}) copy-start(s32[1,2,64]{2,1,0:T(2,128)} %param.9) | copy-start | bytes 1540
  46.3 25.3 %collective-permute-start.9 = (bf16[8192,128]{1,0:T(8,128)(2,1)S(1)}, bf16[8192,128]{1,0:T(8,128)(2,1)S(1)}, u32[]{:S(2)}, u32[]{:S(2)}) collective-permute-start(bf16[8192,128]{1,0:T(8,128)(2,1)S(1)} %constant_dynamic-update-slice_fusion), channel_id=1, source_target_pairs={{0,16},{16,0},{1,17},{17,1},{2,18},{18,2},{3,19},{19,3},{4,20},{20... | collective-permute-start | bytes 6291464 | tf_op jit(solution)/shard_map/ppermute | solution.py:200
  48.3 16.4 %collective-permute-start.8 = (bf16[16,8320]{1,0:T(8,128)(2,1)S(1)}, bf16[16,8320]{1,0:T(8,128)(2,1)}, u32[]{:S(2)}, u32[]{:S(2)}) collective-permute-start(bf16[16,8320]{1,0:T(8,128)(2,1)S(1)} %collective-permute-done.3.refs_4_), channel_id=1, source_target_pairs={{0,14},{2,0},{4,2},{6,4},{8,6},{10,8},{12,10},{14,12},{16,18},{18,... | collective-permute-start | bytes 798728 | tf_op jit(solution)/shard_map/ppermute | solution.py:169
  54.8 16.8 %collective-permute-start.7 = (bf16[16,8320]{1,0:T(8,128)(2,1)S(1)}, bf16[16,8320]{1,0:T(8,128)(2,1)S(1)}, u32[]{:S(2)}, u32[]{:S(2)}) collective-permute-start(bf16[16,8320]{1,0:T(8,128)(2,1)S(1)} %collective-permute-done.1.refs_5_), channel_id=1, source_target_pairs={{0,2},{2,4},{4,6},{6,8},{8,10},{10,12},{12,14},{14,0},{16,30},{18,... | collective-permute-start | bytes 798728 | tf_op jit(solution)/shard_map/ppermute | solution.py:169
  64.7 17.6 %collective-permute-start.10 = (bf16[16,8320]{1,0:T(8,128)(2,1)}, bf16[16,8320]{1,0:T(8,128)(2,1)}, u32[]{:S(2)}, u32[]{:S(2)}) collective-permute-start(bf16[16,8320]{1,0:T(8,128)(2,1)} %collective-permute-done.8.refs_6_), channel_id=1, source_target_pairs={{0,14},{2,0},{4,2},{6,4},{8,6},{10,8},{12,10},{14,12},{16,18},{18,... | collective-permute-start | bytes 798728 | tf_op jit(solution)/shard_map/ppermute | solution.py:169
  71.6 1.3 %copy-start = (bf16[8192,128]{1,0:T(8,128)(2,1)}, bf16[8192,128]{1,0:T(8,128)(2,1)S(1)}, u32[]{:S(2)}) copy-start(bf16[8192,128]{1,0:T(8,128)(2,1)S(1)} %collective-permute-done.9) | copy-start | bytes 6291460
  72.9 12.5 %collective-permute-start.11 = (bf16[16,8320]{1,0:T(8,128)(2,1)S(1)}, bf16[16,8320]{1,0:T(8,128)(2,1)}, u32[]{:S(2)}, u32[]{:S(2)}) collective-permute-start(bf16[16,8320]{1,0:T(8,128)(2,1)S(1)} %collective-permute-done.7.refs_2_), channel_id=1, source_target_pairs={{0,2},{2,4},{4,6},{6,8},{8,10},{10,12},{12,14},{14,0},{16,30},{18,... | collective-permute-start | bytes 798728 | tf_op jit(solution)/shard_map/ppermute | solution.py:169
  75.2 1.6 %copy-start.1 = (bf16[8192,128]{1,0:T(8,128)(2,1)S(1)}, bf16[8192,128]{1,0:T(8,128)(2,1)}, u32[]{:S(2)}) copy-start(bf16[8192,128]{1,0:T(8,128)(2,1)} %copy-done) | copy-start | bytes 6291460

commit v7 on v4

--- a/solution.py
+++ b/solution.py
@@ -188,7 +188,7 @@
     back.append(turn(back[2], -1))
     mine = jnp.concatenate([mine] + moved, axis=0)
     other = lax.ppermute(mine, "core", [(0, 1), (1, 0)])
-    fwd[3], back[2], other = after(fwd[3], back[2], other)
+    fwd[3], back[2] = after(fwd[3], back[2])
     b = [v.reshape(-1, BLK, width) for v in (mine, other)]
     far_end = turn(fwd[3], 1)
 

time: 106 us -> 106 us (level)
  the two profiles are of different devices: /device:TPU:2 before, /device:TPU:1 now
where the time goes in v7:
time: 106 us; the launch traced here: 105 us
  starting transfers between devices  48 us (45%)
  waiting for transfers between devices  22.7 us (21%)
  blocking collectives  19.7 us (19%)
  Pallas kernels  12.2 us (12%)
  local copies, waits for them, and re-layouts  1.4 us (1%)
    ppermute x7, starting transfers between devices, turn(): return lax.ppermute(v, ('core', 'zb'), pairs)  32 us
    all_to_all x1, blocking collectives, body(): out = lax.all_to_all(out, ('layer', 'zc'), 0, 0, tiled=True)  19.7 us
    ppermute x7, waiting for transfers between devices, turn(): return lax.ppermute(v, ('core', 'zb'), pairs)  16.3 us
    ppermute x3, starting transfers between devices, body(): lax.ppermute(mine, 'x', [(i, (i - k) % nx) for i in range(nx)])  9.33 us
    pallas_call x2, Pallas kernels, product(): pl.pallas_call(functools.partial(product_kernel, parts=parts, brows=brows...  8.78 us
    ppermute x3, waiting for transfers between devices, body(): lax.ppermute(mine, 'x', [(i, (i - k) % nx) for i in range(nx)])  6.44 us
    ppermute x1, starting transfers between devices, body(): far = lax.ppermute(mine, 'zc', [(0, 1), (1, 0)])  4.37 us
    ppermute x1, starting transfers between devices, body(): other = lax.ppermute(mine, 'core', [(0, 1), (1, 0)])  2.34 us
  transfers between devices with their start and end apart: 12, of which 7 were waited for; matrix products, arithmetic and copies ran while one was open for 2% of the time, Pallas kernels for 6%

profile of v7, /device:TPU:1, one launch (start us, length us, event | category | flops | bytes accessed | tf_op | source)
XLA Modules:
  0.0 105.3 jit_solution(14342486568022811562)
XLA Ops:
  0.0 4.4 %collective-permute-start.2 = (bf16[1024,128]{1,0:T(8,128)(2,1)}, bf16[1024,128]{1,0:T(8,128)(2,1)S(1)}, u32[]{:S(2)}, u32[]{:S(2)}) collective-permute-start(bf16[1024,128]{1,0:T(8,128)(2,1)} %bitcast.22), channel_id=1, source_target_pairs={{0,1},{1,0},{2,3},{3,2},{4,5},{5,4},{6,7},{7,6},{8,9},{9,8},{10,11... | collective-permute-start | bytes 786440 | tf_op jit(solution)/shard_map/ppermute | solution.py:176
  4.4 1.7 %pack.1.refs_2_ = bf16[16,8320]{1,0:T(8,128)(2,1)} custom-call(bf16[2,16,4096]{2,1,0:T(8,128)(2,1)} %bitcast.25, s32[2,16]{1,0:T(2,128)} %bitcast.26, s32[2]{0:T(128)} %bitcast.27), custom_call_target="tpu_custom_call" | custom-call | tf_op jit(solution)/shard_map/pack/pallas_call | solution.py:161
  6.1 10.7 %collective-permute-start = (bf16[16,8320]{1,0:T(8,128)(2,1)}, bf16[16,8320]{1,0:T(8,128)(2,1)S(1)}, u32[]{:S(2)}, u32[]{:S(2)}) collective-permute-start(bf16[16,8320]{1,0:T(8,128)(2,1)} %pack.1.refs_2_), channel_id=1, source_target_pairs={{0,2},{2,4},{4,6},{6,8},{8,10},{10,12},{12,14},{14,0},{16,30},{18,... | collective-permute-start | bytes 798728 | tf_op jit(solution)/shard_map/ppermute | solution.py:159
  16.7 1.0 pad_maximum_fusion
  17.7 4.4 %collective-permute-start.4 = (bf16[2048,128]{1,0:T(8,128)(2,1)S(1)}, bf16[2048,128]{1,0:T(8,128)(2,1)S(1)}, u32[]{:S(2)}, u32[]{:S(2)}) collective-permute-start(bf16[2048,128]{1,0:T(8,128)(2,1)S(1)} %pad_maximum_fusion), channel_id=1, source_target_pairs={{0,96},{32,0},{64,32},{96,64},{1,97},{33,1},{65,33},{97,65},{2,98}... | collective-permute-start | bytes 1572872 | tf_op jit(solution)/shard_map/ppermute | solution.py:180
  22.1 2.4 %collective-permute-start.5 = (bf16[2048,128]{1,0:T(8,128)(2,1)S(1)}, bf16[2048,128]{1,0:T(8,128)(2,1)S(1)}, u32[]{:S(2)}, u32[]{:S(2)}) collective-permute-start(bf16[2048,128]{1,0:T(8,128)(2,1)S(1)} %pad_maximum_fusion), channel_id=1, source_target_pairs={{0,64},{32,96},{64,0},{96,32},{1,65},{33,97},{65,1},{97,33},{2,66}... | collective-permute-start | bytes 1572872 | tf_op jit(solution)/shard_map/ppermute | solution.py:180
  24.6 2.5 %collective-permute-start.6 = (bf16[2048,128]{1,0:T(8,128)(2,1)S(1)}, bf16[2048,128]{1,0:T(8,128)(2,1)S(1)}, u32[]{:S(2)}, u32[]{:S(2)}) collective-permute-start(bf16[2048,128]{1,0:T(8,128)(2,1)S(1)} %pad_maximum_fusion), channel_id=1, source_target_pairs={{0,32},{32,64},{64,96},{96,0},{1,33},{33,65},{65,97},{97,1},{2,34}... | collective-permute-start | bytes 1572872 | tf_op jit(solution)/shard_map/ppermute | solution.py:180
  27.1 1.9 %collective-permute-start.3 = (bf16[16,8320]{1,0:T(8,128)(2,1)}, bf16[16,8320]{1,0:T(8,128)(2,1)S(1)}, u32[]{:S(2)}, u32[]{:S(2)}) collective-permute-start(bf16[16,8320]{1,0:T(8,128)(2,1)} %pack.1.refs_2_), channel_id=1, source_target_pairs={{0,14},{2,0},{4,2},{6,4},{8,6},{10,8},{12,10},{14,12},{16,18},{18,... | collective-permute-start | bytes 798728 | tf_op jit(solution)/shard_map/ppermute | solution.py:159
  29.0 5.5 %collective-permute-start.1 = (bf16[16,8320]{1,0:T(8,128)(2,1)S(1)}, bf16[16,8320]{1,0:T(8,128)(2,1)S(1)}, u32[]{:S(2)}, u32[]{:S(2)}) collective-permute-start(bf16[16,8320]{1,0:T(8,128)(2,1)S(1)} %collective-permute-done.refs_3_), channel_id=1, source_target_pairs={{0,2},{2,4},{4,6},{6,8},{8,10},{10,12},{12,14},{14,0},{16,30},{18,... | collective-permute-start | bytes 798728 | tf_op jit(solution)/shard_map/ppermute | solution.py:159
  34.5 1.0 constant_dynamic-update-slice_fusion.4
  35.5 2.5 %collective-permute-done.3.refs_4_ = bf16[16,8320]{1,0:T(8,128)(2,1)S(1)} collective-permute-done((bf16[16,8320]{1,0:T(8,128)(2,1)}, bf16[16,8320]{1,0:T(8,128)(2,1)S(1)}, u32[]{:S(2)}, u32[]{:S(2)}) %collective-permute-start.3) | collective-permute-done | bytes 266272 | tf_op jit(solution)/shard_map/ppermute | solution.py:159
  38.0 5.6 %collective-permute-done.1.refs_5_ = bf16[16,8320]{1,0:T(8,128)(2,1)S(1)} collective-permute-done((bf16[16,8320]{1,0:T(8,128)(2,1)S(1)}, bf16[16,8320]{1,0:T(8,128)(2,1)S(1)}, u32[]{:S(2)}, u32[]{:S(2)}) %collective-permute-start.1) | collective-permute-done | bytes 266272 | tf_op jit(solution)/shard_map/ppermute | solution.py:159
  44.3 5.9 %collective-permute-done.6 = bf16[2048,128]{1,0:T(8,128)(2,1)S(1)} collective-permute-done((bf16[2048,128]{1,0:T(8,128)(2,1)S(1)}, bf16[2048,128]{1,0:T(8,128)(2,1)S(1)}, u32[]{:S(2)}, u32[]{:S(2)}) %collective-permute-start.6) | collective-permute-done | bytes 524320 | tf_op jit(solution)/shard_map/ppermute | solution.py:180
  50.3 2.3 %collective-permute-start.11 = (bf16[8192,128]{1,0:T(8,128)(2,1)S(1)}, bf16[8192,128]{1,0:T(8,128)(2,1)}, u32[]{:S(2)}, u32[]{:S(2)}) collective-permute-start(bf16[8192,128]{1,0:T(8,128)(2,1)S(1)} %constant_dynamic-update-slice_fusion), channel_id=1, source_target_pairs={{0,16},{16,0},{1,17},{17,1},{2,18},{18,2},{3,19},{19,3},{4,20},{20... | collective-permute-start | bytes 6291464 | tf_op jit(solution)/shard_map/ppermute | solution.py:190
  52.7 1.9 %collective-permute-start.8 = (bf16[16,8320]{1,0:T(8,128)(2,1)S(1)}, bf16[16,8320]{1,0:T(8,128)(2,1)}, u32[]{:S(2)}, u32[]{:S(2)}) collective-permute-start(bf16[16,8320]{1,0:T(8,128)(2,1)S(1)} %collective-permute-done.3.refs_4_), channel_id=1, source_target_pairs={{0,14},{2,0},{4,2},{6,4},{8,6},{10,8},{12,10},{14,12},{16,18},{18,... | collective-permute-start | bytes 798728 | tf_op jit(solution)/shard_map/ppermute | solution.py:159
  54.6 5.5 %collective-permute-start.7 = (bf16[16,8320]{1,0:T(8,128)(2,1)S(1)}, bf16[16,8320]{1,0:T(8,128)(2,1)S(1)}, u32[]{:S(2)}, u32[]{:S(2)}) collective-permute-start(bf16[16,8320]{1,0:T(8,128)(2,1)S(1)} %collective-permute-done.1.refs_5_), channel_id=1, source_target_pairs={{0,2},{2,4},{4,6},{6,8},{8,10},{10,12},{12,14},{14,0},{16,30},{18,... | collective-permute-start | bytes 798728 | tf_op jit(solution)/shard_map/ppermute | solution.py:159
  60.1 2.6 %collective-permute-done.8.refs_6_ = bf16[16,8320]{1,0:T(8,128)(2,1)} collective-permute-done((bf16[16,8320]{1,0:T(8,128)(2,1)S(1)}, bf16[16,8320]{1,0:T(8,128)(2,1)}, u32[]{:S(2)}, u32[]{:S(2)}) %collective-permute-start.8) | collective-permute-done | bytes 266272 | tf_op jit(solution)/shard_map/ppermute | solution.py:159
  62.7 1.9 %collective-permute-start.9 = (bf16[16,8320]{1,0:T(8,128)(2,1)}, bf16[16,8320]{1,0:T(8,128)(2,1)}, u32[]{:S(2)}, u32[]{:S(2)}) collective-permute-start(bf16[16,8320]{1,0:T(8,128)(2,1)} %collective-permute-done.8.refs_6_), channel_id=1, source_target_pairs={{0,14},{2,0},{4,2},{6,4},{8,6},{10,8},{12,10},{14,12},{16,18},{18,... | collective-permute-start | bytes 798728 | tf_op jit(solution)/shard_map/ppermute | solution.py:159
  64.6 5.2 %collective-permute-done.7.refs_2_ = bf16[16,8320]{1,0:T(8,128)(2,1)S(1)} collective-permute-done((bf16[16,8320]{1,0:T(8,128)(2,1)S(1)}, bf16[16,8320]{1,0:T(8,128)(2,1)S(1)}, u32[]{:S(2)}, u32[]{:S(2)}) %collective-permute-start.7) | collective-permute-done | bytes 266272 | tf_op jit(solution)/shard_map/ppermute | solution.py:159
  69.8 4.6 %collective-permute-start.10 = (bf16[16,8320]{1,0:T(8,128)(2,1)S(1)}, bf16[16,8320]{1,0:T(8,128)(2,1)}, u32[]{:S(2)}, u32[]{:S(2)}) collective-permute-start(bf16[16,8320]{1,0:T(8,128)(2,1)S(1)} %collective-permute-done.7.refs_2_), channel_id=1, source_target_pairs={{0,2},{2,4},{4,6},{6,8},{8,10},{10,12},{12,14},{14,0},{16,30},{18,... | collective-permute-start | bytes 798728 | tf_op jit(solution)/shard_map/ppermute | solution.py:159
  74.8 4.9 %product.1.refs_7_ = f32[4,256,128]{2,1,0:T(8,128)S(1)} custom-call(s32[2,64]{1,0:T(2,128)S(1)} %bitcast.20, s32[8]{0:T(128)S(1)} %stack.54.refs_1_, bf16[16,8320]{1,0:T(8,128)(2,1)S(1)} %copy-done, bf16[16,8320]{1,0:T(8,128)(2,1)S(1)} %collective-permute-done.refs_3_, bf16[16,8320]{1,0:T(8,128)(2,1)S(1)} %collective-permute-done.3.refs_4_, ...), custom_call_target="tpu_custom_call" | custom-call | flops 1342177280 | bytes 8388608 | tf_op jit(solution)/shard_map/product/pallas_call | solution.py:111
  80.1 3.8 %product_last.1 = f32[8,64,256]{2,1,0:T(8,128)S(1)} custom-call(s32[2,64]{1,0:T(2,128)S(1)} %bitcast.21, s32[6]{0:T(128)S(1)} %stack.48.refs_1_, bf16[16,8320]{1,0:T(8,128)(2,1)S(1)} %collective-permute-done.7.refs_2_, bf16[16,8320]{1,0:T(8,128)(2,1)} %collective-permute-done.9.refs_3_, bf16[16,8320]{1,0:T(8,128)(2,1)} %collective-permute-done.10.refs_4_, ...), custom_call_target="tpu_custom_call" | custom-call | flops 805306368 | bytes 8388608 | tf_op jit(solution)/shard_map/product_last/pallas_call | solution.py:111
  83.9 19.7 %all_to_all.5.parts_ref = f32[8,64,256]{2,1,0:T(8,128)} all-to-all(f32[8,64,256]{2,1,0:T(8,128)S(1)} %product_last.1), channel_id=1, replica_groups=mesh['layer'=4,'x'=4,'core'=2,'zb'=8,'zc'=2] {'layer','zc'}, dimensions={0} | all-to-all | bytes 1048576 | tf_op jit(solution)/shard_map/all_to_all | solution.py:213
  103.6 1.7 %finish.1 = bf16[128,128]{1,0:T(8,128)(2,1)} custom-call(f32[8,64,256]{2,1,0:T(8,128)} %all_to_all.5.parts_ref), custom_call_target="tpu_custom_call" | custom-call | tf_op jit(solution)/shard_map/finish/pallas_call | solution.py:214
  (17 shorter events, 1.3 us)
Async XLA Ops:
  0.0 16.7 %collective-permute-start.2 = (bf16[1024,128]{1,0:T(8,128)(2,1)}, bf16[1024,128]{1,0:T(8,128)(2,1)S(1)}, u32[]{:S(2)}, u32[]{:S(2)}) collective-permute-start(bf16[1024,128]{1,0:T(8,128)(2,1)} %bitcast.22), channel_id=1, source_target_pairs={{0,1},{1,0},{2,3},{3,2},{4,5},{5,4},{6,7},{7,6},{8,9},{9,8},{10,11... | collective-permute-start | bytes 786440 | tf_op jit(solution)/shard_map/ppermute | solution.py:176
  6.1 22.9 %collective-permute-start = (bf16[16,8320]{1,0:T(8,128)(2,1)}, bf16[16,8320]{1,0:T(8,128)(2,1)S(1)}, u32[]{:S(2)}, u32[]{:S(2)}) collective-permute-start(bf16[16,8320]{1,0:T(8,128)(2,1)} %pack.1.refs_2_), channel_id=1, source_target_pairs={{0,2},{2,4},{4,6},{6,8},{8,10},{10,12},{12,14},{14,0},{16,30},{18,... | collective-permute-start | bytes 798728 | tf_op jit(solution)/shard_map/ppermute | solution.py:159
  17.7 26.5 %collective-permute-start.4 = (bf16[2048,128]{1,0:T(8,128)(2,1)S(1)}, bf16[2048,128]{1,0:T(8,128)(2,1)S(1)}, u32[]{:S(2)}, u32[]{:S(2)}) collective-permute-start(bf16[2048,128]{1,0:T(8,128)(2,1)S(1)} %pad_maximum_fusion), channel_id=1, source_target_pairs={{0,96},{32,0},{64,32},{96,64},{1,97},{33,1},{65,33},{97,65},{2,98}... | collective-permute-start | bytes 1572872 | tf_op jit(solution)/shard_map/ppermute | solution.py:180
  22.1 22.1 %collective-permute-start.5 = (bf16[2048,128]{1,0:T(8,128)(2,1)S(1)}, bf16[2048,128]{1,0:T(8,128)(2,1)S(1)}, u32[]{:S(2)}, u32[]{:S(2)}) collective-permute-start(bf16[2048,128]{1,0:T(8,128)(2,1)S(1)} %pad_maximum_fusion), channel_id=1, source_target_pairs={{0,64},{32,96},{64,0},{96,32},{1,65},{33,97},{65,1},{97,33},{2,66}... | collective-permute-start | bytes 1572872 | tf_op jit(solution)/shard_map/ppermute | solution.py:180
  24.6 25.6 %collective-permute-start.6 = (bf16[2048,128]{1,0:T(8,128)(2,1)S(1)}, bf16[2048,128]{1,0:T(8,128)(2,1)S(1)}, u32[]{:S(2)}, u32[]{:S(2)}) collective-permute-start(bf16[2048,128]{1,0:T(8,128)(2,1)S(1)} %pad_maximum_fusion), channel_id=1, source_target_pairs={{0,32},{32,64},{64,96},{96,0},{1,33},{33,65},{65,97},{97,1},{2,34}... | collective-permute-start | bytes 1572872 | tf_op jit(solution)/shard_map/ppermute | solution.py:180
  27.1 10.9 %collective-permute-start.3 = (bf16[16,8320]{1,0:T(8,128)(2,1)}, bf16[16,8320]{1,0:T(8,128)(2,1)S(1)}, u32[]{:S(2)}, u32[]{:S(2)}) collective-permute-start(bf16[16,8320]{1,0:T(8,128)(2,1)} %pack.1.refs_2_), channel_id=1, source_target_pairs={{0,14},{2,0},{4,2},{6,4},{8,6},{10,8},{12,10},{14,12},{16,18},{18,... | collective-permute-start | bytes 798728 | tf_op jit(solution)/shard_map/ppermute | solution.py:159
  29.0 14.7 %collective-permute-start.1 = (bf16[16,8320]{1,0:T(8,128)(2,1)S(1)}, bf16[16,8320]{1,0:T(8,128)(2,1)S(1)}, u32[]{:S(2)}, u32[]{:S(2)}) collective-permute-start(bf16[16,8320]{1,0:T(8,128)(2,1)S(1)} %collective-permute-done.refs_3_), channel_id=1, source_target_pairs={{0,2},{2,4},{4,6},{6,8},{8,10},{10,12},{12,14},{14,0},{16,30},{18,... | collective-permute-start | bytes 798728 | tf_op jit(solution)/shard_map/ppermute | solution.py:159
  35.5 39.3 %copy-start = (bf16[16,8320]{1,0:T(8,128)(2,1)S(1)}, bf16[16,8320]{1,0:T(8,128)(2,1)}, u32[]{:S(2)}) copy-start(bf16[16,8320]{1,0:T(8,128)(2,1)} %pack.1.refs_2_) | copy-start | bytes 798724
  35.5 39.3 %copy-start.1 = (s32[1,2,64]{2,1,0:T(2,128)S(1)}, s32[1,2,64]{2,1,0:T(2,128)}, u32[]{:S(2)}) copy-start(s32[1,2,64]{2,1,0:T(2,128)} %param.9) | copy-start | bytes 1540
  50.3 24.4 %collective-permute-start.11 = (bf16[8192,128]{1,0:T(8,128)(2,1)S(1)}, bf16[8192,128]{1,0:T(8,128)(2,1)}, u32[]{:S(2)}, u32[]{:S(2)}) collective-permute-start(bf16[8192,128]{1,0:T(8,128)(2,1)S(1)} %constant_dynamic-update-slice_fusion), channel_id=1, source_target_pairs={{0,16},{16,0},{1,17},{17,1},{2,18},{18,2},{3,19},{19,3},{4,20},{20... | collective-permute-start | bytes 6291464 | tf_op jit(solution)/shard_map/ppermute | solution.py:190
  52.7 10.0 %collective-permute-start.8 = (bf16[16,8320]{1,0:T(8,128)(2,1)S(1)}, bf16[16,8320]{1,0:T(8,128)(2,1)}, u32[]{:S(2)}, u32[]{:S(2)}) collective-permute-start(bf16[16,8320]{1,0:T(8,128)(2,1)S(1)} %collective-permute-done.3.refs_4_), channel_id=1, source_target_pairs={{0,14},{2,0},{4,2},{6,4},{8,6},{10,8},{12,10},{14,12},{16,18},{18,... | collective-permute-start | bytes 798728 | tf_op jit(solution)/shard_map/ppermute | solution.py:159
  54.6 15.2 %collective-permute-start.7 = (bf16[16,8320]{1,0:T(8,128)(2,1)S(1)}, bf16[16,8320]{1,0:T(8,128)(2,1)S(1)}, u32[]{:S(2)}, u32[]{:S(2)}) collective-permute-start(bf16[16,8320]{1,0:T(8,128)(2,1)S(1)} %collective-permute-done.1.refs_5_), channel_id=1, source_target_pairs={{0,2},{2,4},{4,6},{6,8},{8,10},{10,12},{12,14},{14,0},{16,30},{18,... | collective-permute-start | bytes 798728 | tf_op jit(solution)/shard_map/ppermute | solution.py:159
  62.7 17.1 %collective-permute-start.9 = (bf16[16,8320]{1,0:T(8,128)(2,1)}, bf16[16,8320]{1,0:T(8,128)(2,1)}, u32[]{:S(2)}, u32[]{:S(2)}) collective-permute-start(bf16[16,8320]{1,0:T(8,128)(2,1)} %collective-permute-done.8.refs_6_), channel_id=1, source_target_pairs={{0,14},{2,0},{4,2},{6,4},{8,6},{10,8},{12,10},{14,12},{16,18},{18,... | collective-permute-start | bytes 798728 | tf_op jit(solution)/shard_map/ppermute | solution.py:159
  69.8 10.3 %collective-permute-start.10 = (bf16[16,8320]{1,0:T(8,128)(2,1)S(1)}, bf16[16,8320]{1,0:T(8,128)(2,1)}, u32[]{:S(2)}, u32[]{:S(2)}) collective-permute-start(bf16[16,8320]{1,0:T(8,128)(2,1)S(1)} %collective-permute-done.7.refs_2_), channel_id=1, source_target_pairs={{0,2},{2,4},{4,6},{6,8},{8,10},{10,12},{12,14},{14,0},{16,30},{18,... | collective-permute-start | bytes 798728 | tf_op jit(solution)/shard_map/ppermute | solution.py:159
